TPU v7x, 256 devices: a whole 4x4x8 slice. The times are simulated.
256 devices in a mesh: band: 8 (over z_hi, x), pw: 32 (over z_lo, y, core).
Axes of the slice: x: 4, y: 4, z: 8 (z_hi: 2, z_lo: 4; z = z_hi * 4 + z_lo), core: 2. Of those that a mesh axis runs over, the one named last changes fastest.
Arguments:
- orbitals: float32 [8, 2, 2, 192, 4096], P('band', None, None, None, 'pw'), may hold values from -6 to 6
- potential: float32 [192, 192, 192], P('pw'), may hold values from -2 to 2
- projectors: float32 [8, 2, 192, 4096], P(None, None, None, 'pw'), may hold values from -6 to 6
- coupling: float32 [8, 8], replicated, may hold values from -0.9 to 0.9
- columns: int32 [4096], P('pw'), may hold values from 0 to 36863, as said below
Outputs:
- applied: float32 [8, 2, 2, 192, 4096], P('band', None, None, None, 'pw')
- cross_terms: float32 [8, 4, 2, 2, 2], P('band')
Inputs may be any that keep to these rules, and one draw needn't show every extreme that they name: Distinct grid columns.
All inputs are finite; a program needn't handle non-finite values.
Results may differ from a plain program's by a relative error of at most 0.0039.
Values may be sent and summed in bfloat16 or wider, within the bound.
No kernel may reach another device: no remote copies, remote signals or barrier semaphores. Data moves between devices by JAX's collectives and lax.ppermute only.
A program may use at most 192 MiB of HBM per device.

v0:
```python
from functools import partial
import math

import jax
import jax.numpy as jnp
from jax import lax
from jax.sharding import PartitionSpec as P

GRID = 192


HIGHEST = lax.Precision.HIGHEST


def from_behind(value, axis, steps):
    count = lax.axis_size(axis)
    initial, last = (max(0, -steps), min(count, count - steps))
    return lax.ppermute(value, axis, [(source, source + steps) for source in range(initial, last)])


def dft_tables(length):
    indices = jnp.arange(length, dtype=jnp.int32)
    phase = indices[:, None] * indices[None, :] % length
    angle = phase.astype(jnp.float32) * (2.0 * math.pi / length)
    factor = 1.0 / math.sqrt(length)
    return (jnp.cos(angle) * factor, jnp.sin(angle) * factor)


def plane_transform(planes, cos_table, sine_table, sign):
    width = cos_table.shape[0]
    y_table = jnp.block([[cos_table, sign * sine_table], [-sign * sine_table, cos_table]])
    along_y = jnp.matmul(planes, y_table, precision=HIGHEST)
    cos_part = jnp.einsum("nk,bdky->bdny", cos_table, along_y, precision=HIGHEST)
    sine_part = jnp.einsum("nk,bdky->bdny", sine_table, along_y, precision=HIGHEST)
    swapped = jnp.concatenate([-sine_part[..., width:], sine_part[..., :width]], axis=-1)
    return cos_part + sign * swapped


def wrapped(freqs):
    return jnp.where(freqs >= GRID // 2, freqs - GRID, freqs)


def middle(planes, potential, all_columns):
    count = planes.shape[0]
    depth = planes.shape[2]
    total_cols = planes.shape[3]
    real_index = all_columns // GRID * (2 * GRID) + all_columns % GRID
    index = jnp.concatenate([real_index, real_index + GRID])
    values = jnp.transpose(planes, (0, 2, 1, 3)).reshape(count, depth, 2 * total_cols)
    flat = jnp.zeros((count, depth, 2 * GRID * GRID), jnp.float32).at[:, :, index].set(values)
    grid = flat.reshape(count, depth, GRID, 2 * GRID)
    cos_table, sine_table = dft_tables(GRID)
    tiled = jnp.concatenate([potential, potential], axis=-1)
    field = plane_transform(grid, cos_table, sine_table, 1.0) * tiled[None]
    back = plane_transform(field, cos_table, sine_table, -1.0).reshape(
        count, depth, 2 * GRID * GRID
    )[:, :, index]
    return jnp.transpose(back.reshape(count, depth, 2, total_cols), (0, 2, 1, 3))


def per_device(orbitals, potential, projectors, coupling, columns):
    block = orbitals[0]
    band_count = block.shape[0]
    local_cols = block.shape[3]
    all_columns = lax.all_gather(columns, "pw", axis=0, tiled=True)
    scale = 1.0 / jnp.sqrt(jnp.float32(all_columns.shape[0] * GRID))
    cos_table, sine_table = dft_tables(GRID)
    inverse_z = jnp.block([[cos_table, -sine_table], [sine_table, cos_table]])
    forward_z = jnp.block([[cos_table, sine_table], [-sine_table, cos_table]])
    flat_block = block.reshape(band_count, 2 * GRID, local_cols)
    zfield = jnp.einsum("pq,bqc->bpc", inverse_z, flat_block, precision=HIGHEST).reshape(
        band_count, 2, GRID, local_cols
    )
    pieces = []
    for band_index in range(band_count):
        sent = lax.all_to_all(
            zfield[band_index : band_index + 1], "pw", split_axis=2, concat_axis=3, tiled=True
        )
        pieces.append(
            lax.all_to_all(
                middle(sent, potential, all_columns), "pw", split_axis=3, concat_axis=2, tiled=True
            )
        )
    returned = jnp.concatenate(pieces, axis=0)
    local_term = jnp.einsum(
        "pq,bqc->bpc",
        forward_z,
        returned.reshape(band_count, 2 * GRID, local_cols),
        precision=HIGHEST,
    ).reshape(band_count, 2, GRID, local_cols)
    wave_x = wrapped(columns // GRID)
    wave_y = wrapped(columns % GRID)
    wave_z = wrapped(jnp.arange(GRID, dtype=jnp.int32))
    squared = wave_z[:, None] * wave_z[:, None] + (wave_x * wave_x + wave_y * wave_y)[None, :]
    kinetic = 4.0 / (GRID * GRID) * squared.astype(jnp.float32)
    beta_real = projectors[:, 0]
    beta_imag = projectors[:, 1]
    wave_real = block[:, 0]
    wave_imag = block[:, 1]
    contract = partial(jnp.einsum, "jzc,bzc->bj", precision=HIGHEST)
    proj_real = contract(beta_real, wave_real) + contract(beta_imag, wave_imag)
    proj_imag = contract(beta_real, wave_imag) - contract(beta_imag, wave_real)
    proj_real, proj_imag = lax.psum((proj_real, proj_imag), "pw")
    coupling_sym = 0.5 * (coupling + coupling.T)
    mixed_real = jnp.matmul(proj_real * scale, coupling_sym, precision=HIGHEST)
    mixed_imag = jnp.matmul(proj_imag * scale, coupling_sym, precision=HIGHEST)
    expand = partial(jnp.einsum, "bk,kzc->bzc", precision=HIGHEST)
    nonlocal_real = expand(mixed_real, beta_real) - expand(mixed_imag, beta_imag)
    nonlocal_imag = expand(mixed_real, beta_imag) + expand(mixed_imag, beta_real)
    nonlocal_term = jnp.stack([nonlocal_real, nonlocal_imag], axis=1)
    applied = local_term + kinetic * block + nonlocal_term
    low_orbitals = block.astype(jnp.bfloat16)
    low_applied = applied.astype(jnp.bfloat16)
    offsets = (-2, -1, 1, 2)
    others = []
    for offset in offsets:
        others.append(from_behind(low_orbitals, "band", -offset))
    terms = []
    for other in others:
        cross_real = jnp.einsum(
            "mtzc,ntzc->mn", other, low_applied, preferred_element_type=jnp.float32
        )
        cross_imag = jnp.einsum(
            "mzc,nzc->mn", other[:, 0], low_applied[:, 1], preferred_element_type=jnp.float32
        ) - jnp.einsum(
            "mzc,nzc->mn", other[:, 1], low_applied[:, 0], preferred_element_type=jnp.float32
        )
        terms.append(jnp.stack([cross_real, cross_imag]))
    summed = lax.psum(jnp.stack(terms), "pw")
    cross_terms = (summed * scale)[None]
    return (applied[None], cross_terms)


def solution(mesh):
    return jax.shard_map(
        per_device,
        mesh=mesh,
        in_specs=(
            P("band", None, None, None, "pw"),
            P("pw", None, None),
            P(None, None, None, "pw"),
            P(),
            P("pw"),
        ),
        out_specs=(P("band", None, None, None, "pw"), P("band", None, None, None, None)),
        check_vma=False,
    )
```

profile of v0, /device:TPU:132, one launch (start us, length us, event | category | flops | bytes accessed | tf_op | source)
XLA Modules:
  0.0 629.7 jit_solution(3100407433693870018)
XLA Ops:
  7.1 4.0 collective-permute-start.2
  11.2 11.5 %collective-permute-start.3 = (bf16[2,2,192,128]{3,0,2,1:T(2,128)(2,1)}, bf16[2,2,192,128]{3,0,2,1:T(2,128)(2,1)}, u32[]{:S(2)}, u32[]{:S(2)}) collective-permute-start(bf16[2,2,192,128]{3,0,2,1:T(2,128)(2,1)} %bitcast.361), channel_id=1, source_target_pairs={{64,0},{96,32},{128,64},{160,96},{192,128},{224,160},{65,1},{97,33... | collective-permute-start | bytes 589832 | tf_op jit(solution)/shard_map/ppermute | solution.py:18
  27.0 6.2 all-to-all-start
  42.8 73.1 %all-reduce = (f32[2,8]{1,0:T(2,128)S(1)}, f32[2,8]{1,0:T(2,128)S(1)}) all-reduce(f32[2,8]{1,0:T(2,128)S(1)} %fusion.28, f32[2,8]{1,0:T(2,128)S(1)} %fusion.29), channel_id=1, replica_groups=mesh['band'=8,'pw'=32] {'pw'}, use_global_device_ids=true, to_apply=%region_2.3 | all-reduce | flops 32 | bytes 256 | tf_op jit(solution)/shard_map/psum | solution.py:103
  118.4 37.4 %all-gather = s32[32,1,128]{2,1,0:T(1,128)S(1)} all-gather(s32[1,1,128]{2,1,0:T(1,128)S(1)} %bitcast.415), channel_id=1, replica_groups=mesh['band'=8,'pw'=32] {'pw'}, dimensions={0}, use_global_device_ids=true | all-gather | bytes 16896 | tf_op jit(solution)/shard_map/all_gather | solution.py:65
  158.9 3.9 all-to-all-start.2
  165.7 36.1 %scatter_custom_fusion = f32[6,73728]{0,1:T(8,128)} fusion(s32[8192]{0:T(1024)S(1)} %bitcast.401, f32[8192,6]{1,0:T(8,128)} %copy.215, f32[]{:T(128)} %constant.65.clone.1), kind=kCustom, calls=%fused_computation.6 | custom fusion | bytes 1769984 | tf_op jit(solution)/shard_map/scatter | solution.py:50
  201.8 21.5 %copy.216 = f32[6,192,384]{2,1,0:T(8,128)} copy(f32[6,192,384]{0,2,1:T(8,128)} %bitcast.367) | data formatting | bytes 3538944 | tf_op jit(solution)/shard_map/reshape.1
  223.3 5.2 fusion.46
  228.5 3.7 convolution_bitcast_fusion.3
  239.0 35.7 %scatter_custom_fusion.1 = f32[6,73728]{0,1:T(8,128)} fusion(s32[8192]{0:T(1024)S(1)} %bitcast.402, f32[8192,6]{1,0:T(8,128)} %copy.224, f32[]{:T(128)} %constant.65.clone.1), kind=kCustom, calls=%fused_computation.4 | custom fusion | bytes 1769984 | tf_op jit(solution)/shard_map/scatter | solution.py:50
  274.7 21.7 %copy.225 = f32[6,192,384]{2,1,0:T(8,128)} copy(f32[6,192,384]{0,2,1:T(8,128)} %bitcast.366) | data formatting | bytes 3538944 | tf_op jit(solution)/shard_map/reshape.28
  296.4 5.2 fusion.44
  310.8 4.4 fusion.6
  318.1 3.9 fusion.14
  322.0 19.2 %copy.258 = f32[1,6,192,384]{1,3,2,0:T(8,128)} copy(f32[1,6,192,384]{3,2,1,0:T(8,128)} %fusion.14) | data formatting | bytes 3538944 | tf_op jit(solution)/shard_map/reshape | solution.py:55
  341.2 39.6 %gather_fusion = f32[8192,6]{1,0:T(8,128)} fusion(f32[6,73728]{0,1:T(8,128)} %bitcast.369, s32[8192]{0:T(1024)S(1)} %broadcast_clamp_fusion), kind=kCustom, calls=%fused_computation | custom fusion | bytes 425984 | tf_op jit(solution)/shard_map/gather | solution.py:55
  380.9 8.7 %copy.298 = f32[1,6,2,4096]{1,2,0,3:T(2,128)} copy(f32[1,6,2,4096]{1,3,2,0:T(8,128)} %bitcast.376) | data formatting | bytes 393216 | tf_op jit(solution)/shard_map/reshape | solution.py:58
  389.6 8.6 %reshape.362 = f32[32,1,1536]{2,1,0:T(1,128)} reshape(f32[4096,1,2,6]{3,2,1,0:T(2,128)} %bitcast.370) | data formatting | bytes 393216
  398.2 7.9 %all-to-all-start.1 = ((f32[32,1,1536]{2,1,0:T(1,128)}), f32[32,1,1536]{2,1,0:T(1,128)S(1)}, u32[]{:S(2)}, u32[]{:S(2)}) async-start(f32[32,1,1536]{2,1,0:T(1,128)} %reshape.362), calls=%async_computation.1 | async-start | bytes 393216 | tf_op jit(solution)/shard_map/all_to_all | solution.py:80
  408.7 4.0 fusion.12
  415.5 3.9 fusion.17
  419.4 19.2 %copy.259 = f32[1,6,192,384]{1,3,2,0:T(8,128)} copy(f32[1,6,192,384]{3,2,1,0:T(8,128)} %fusion.17) | data formatting | bytes 3538944 | tf_op jit(solution)/shard_map/reshape | solution.py:55
  438.6 39.6 %gather_fusion.1 = f32[8192,6]{1,0:T(8,128)} fusion(f32[6,73728]{0,1:T(8,128)} %bitcast.368, s32[8192]{0:T(1024)S(1)} %broadcast_clamp_fusion), kind=kCustom, calls=%fused_computation.1 | custom fusion | bytes 425984 | tf_op jit(solution)/shard_map/gather | solution.py:55
  478.3 8.7 %copy.299 = f32[1,6,2,4096]{1,2,0,3:T(2,128)} copy(f32[1,6,2,4096]{1,3,2,0:T(8,128)} %bitcast.375) | data formatting | bytes 393216 | tf_op jit(solution)/shard_map/reshape | solution.py:58
  487.0 8.6 %reshape.360 = f32[32,1,1536]{2,1,0:T(1,128)} reshape(f32[4096,1,2,6]{3,2,1,0:T(2,128)} %bitcast.371) | data formatting | bytes 393216
  495.7 8.1 %all-to-all-start.3 = ((f32[32,1,1536]{2,1,0:T(1,128)}), f32[32,1,1536]{2,1,0:T(1,128)S(1)}, u32[]{:S(2)}, u32[]{:S(2)}) async-start(f32[32,1,1536]{2,1,0:T(1,128)} %reshape.360), calls=%async_computation.3 | async-start | bytes 393216 | tf_op jit(solution)/shard_map/all_to_all | solution.py:80
  506.6 7.9 %reshape.363 = f32[4096,1,2,6]{3,2,1,0:T(2,128)} reshape(f32[32,1536]{1,0:T(8,128)S(1)} %reduce.1) | data formatting | bytes 393216
  514.5 5.2 copy.219
  521.1 7.9 %reshape.361 = f32[4096,1,2,6]{3,2,1,0:T(2,128)} reshape(f32[32,1536]{1,0:T(8,128)S(1)} %reduce) | data formatting | bytes 393216
  529.0 5.2 copy.228
  554.3 73.0 %psum.23 = f32[4,2,2,2]{0,3,2,1:T(2,128)S(1)} all-reduce(f32[4,2,2,2]{0,3,2,1:T(2,128)S(1)} %pad_maximum_fusion.8), channel_id=1, replica_groups=mesh['band'=8,'pw'=32] {'pw'}, use_global_device_ids=true, to_apply=%region_4.5 | all-reduce | flops 32 | bytes 256 | tf_op jit(solution)/shard_map/psum | solution.py:129
  (113 shorter events, 79.3 us)
Async XLA Ops:
  2.6 30.6 %copy-start = (f32[1,2,2,192,128]{4,3,2,1,0:T(8,128)S(1)}, f32[1,2,2,192,128]{4,3,2,1,0:T(8,128)}, u32[]{:S(2)}) copy-start(f32[1,2,2,192,128]{4,3,2,1,0:T(8,128)} %param.5) | copy-start | bytes 1179652
  2.6 533.8 %collective-permute-start = (bf16[2,2,192,128]{3,0,2,1:T(2,128)(2,1)}, bf16[2,2,192,128]{3,0,2,1:T(2,128)(2,1)}, u32[]{:S(2)}, u32[]{:S(2)}) collective-permute-start(bf16[2,2,192,128]{3,0,2,1:T(2,128)(2,1)} %bitcast.361), channel_id=1, source_target_pairs={{0,64},{32,96},{64,128},{96,160},{128,192},{160,224},{1,65},{33,97... | collective-permute-start | bytes 589832 | tf_op jit(solution)/shard_map/ppermute | solution.py:18
  4.0 536.8 %collective-permute-start.1 = (bf16[2,2,192,128]{3,0,2,1:T(2,128)(2,1)}, bf16[2,2,192,128]{3,0,2,1:T(2,128)(2,1)}, u32[]{:S(2)}, u32[]{:S(2)}) collective-permute-start(bf16[2,2,192,128]{3,0,2,1:T(2,128)(2,1)} %bitcast.361), channel_id=1, source_target_pairs={{0,32},{32,64},{64,96},{96,128},{128,160},{160,192},{192,224},{1,3... | collective-permute-start | bytes 589832 | tf_op jit(solution)/shard_map/ppermute | solution.py:18
  7.1 538.1 %collective-permute-start.2 = (bf16[2,2,192,128]{3,0,2,1:T(2,128)(2,1)}, bf16[2,2,192,128]{3,0,2,1:T(2,128)(2,1)}, u32[]{:S(2)}, u32[]{:S(2)}) collective-permute-start(bf16[2,2,192,128]{3,0,2,1:T(2,128)(2,1)} %bitcast.361), channel_id=1, source_target_pairs={{32,0},{64,32},{96,64},{128,96},{160,128},{192,160},{224,192},{33,... | collective-permute-start | bytes 589832 | tf_op jit(solution)/shard_map/ppermute | solution.py:18
  11.2 538.6 %collective-permute-start.3 = (bf16[2,2,192,128]{3,0,2,1:T(2,128)(2,1)}, bf16[2,2,192,128]{3,0,2,1:T(2,128)(2,1)}, u32[]{:S(2)}, u32[]{:S(2)}) collective-permute-start(bf16[2,2,192,128]{3,0,2,1:T(2,128)(2,1)} %bitcast.361), channel_id=1, source_target_pairs={{64,0},{96,32},{128,64},{160,96},{192,128},{224,160},{65,1},{97,33... | collective-permute-start | bytes 589832 | tf_op jit(solution)/shard_map/ppermute | solution.py:18
  27.0 131.9 %all-to-all-start = ((f32[1,2,192,128]{3,1,0,2:T(2,128)}), f32[1,2,192,128]{3,1,0,2:T(2,128)S(1)}, u32[]{:S(2)}, u32[]{:S(2)}) async-start(f32[1,2,192,128]{3,1,0,2:T(2,128)} %copy.212), calls=%async_computation | async-start | bytes 393216 | tf_op jit(solution)/shard_map/all_to_all | solution.py:76
  35.0 7.7 %copy-start.6 = (f32[8,8]{1,0:T(8,128)S(1)}, f32[8,8]{1,0:T(8,128)}, u32[]{:S(2)}) copy-start(f32[8,8]{1,0:T(8,128)} %param.8) | copy-start | bytes 772
  38.9 79.5 %copy-start.7 = (s32[128]{0:T(128)S(1)}, s32[128]{0:T(128)}, u32[]{:S(2)}) copy-start(s32[128]{0:T(128)} %param.9) | copy-start | bytes 1540
  158.9 77.1 %all-to-all-start.2 = ((f32[1,2,192,128]{3,1,0,2:T(2,128)}), f32[1,2,192,128]{3,1,0,2:T(2,128)S(1)}, u32[]{:S(2)}, u32[]{:S(2)}) async-start(f32[1,2,192,128]{3,1,0,2:T(2,128)} %copy.221), calls=%async_computation.2 | async-start | bytes 393216 | tf_op jit(solution)/shard_map/all_to_all | solution.py:76
  305.3 3.6 copy-start.1
  309.0 1.5 copy-start.3
  309.0 1.8 copy-start.4
  398.2 97.4 %all-to-all-start.1 = ((f32[32,1,1536]{2,1,0:T(1,128)}), f32[32,1,1536]{2,1,0:T(1,128)S(1)}, u32[]{:S(2)}, u32[]{:S(2)}) async-start(f32[32,1,1536]{2,1,0:T(1,128)} %reshape.362), calls=%async_computation.1 | async-start | bytes 393216 | tf_op jit(solution)/shard_map/all_to_all | solution.py:80
  406.1 2.2 copy-start.2
  406.2 2.5 copy-start.5
  495.7 24.4 %all-to-all-start.3 = ((f32[32,1,1536]{2,1,0:T(1,128)}), f32[32,1,1536]{2,1,0:T(1,128)S(1)}, u32[]{:S(2)}, u32[]{:S(2)}) async-start(f32[32,1,1536]{2,1,0:T(1,128)} %reshape.360), calls=%async_computation.3 | async-start | bytes 393216 | tf_op jit(solution)/shard_map/all_to_all | solution.py:80
where the time goes:
time: 639 us; the launch traced here: 630 us
  local copies, waits for them, and re-layouts  310 us (49%)
  blocking collectives  183 us (29%)
  matrix products  78.2 us (12%)
  starting transfers between devices  46.1 us (7%)
  other arithmetic  10.2 us (2%)
    gather x2, local copies, waits for them, and re-layouts, middle(): plane_transform(field, cos_table, sine_table, -1.0)  79.3 us
    psum x1, blocking collectives, per_device(): proj_real, proj_imag = lax.psum((proj_real, proj_imag), 'pw')  73.1 us
    psum x1, blocking collectives, per_device(): summed = lax.psum(jnp.stack(terms), 'pw')  73 us
    scatter x2, local copies, waits for them, and re-layouts, middle(): jnp.zeros((count, depth, 2 * GRID * GRID), jnp.float32).at[:, :, index]  71.8 us
    another operation x2, local copies, waits for them, and re-layouts  43.2 us
    reshape x2, local copies, waits for them, and re-layouts, middle(): plane_transform(field, cos_table, sine_table, -1.0)  38.4 us
    unnamed x26, local copies, waits for them, and re-layouts  38.1 us
    all_gather x1, blocking collectives, per_device(): all_columns = lax.all_gather(columns, 'pw', axis=0, tiled=True)  37.4 us
  transfers between devices with their start and end apart: 8, of which 0 were waited for; matrix products, arithmetic and copies ran while one was open for 62% of the time, Pallas kernels for 0%

commit v1 on v0

v1 whole, which is shorter than its diff:
```python
from functools import partial
import math

import jax
import jax.numpy as jnp
import numpy as np
from jax import lax
from jax.experimental import pallas as pl
from jax.experimental.pallas import tpu as pltpu
from jax.sharding import PartitionSpec as P

GRID = 192
BANDS = 2
PROJ = 8
PW = 32
LOCAL = 128
COLS = PW * LOCAL
DEPTH = GRID // PW
ROWS = 16
GROUPS = 4
SPAN = GRID // GROUPS
LANES = 128
WIDTH = LANES // GROUPS
BF = jnp.bfloat16
F32 = jnp.float32
HIGHEST = lax.Precision.HIGHEST


def dft_tables():
    index = np.arange(GRID)
    angle = (index[:, None] * index[None, :] % GRID) * (2.0 * math.pi / GRID)
    factor = 1.0 / math.sqrt(GRID)
    return np.cos(angle) * factor, np.sin(angle) * factor


def build_tables():
    cos, sin = dft_tables()
    inverse = np.block([[cos, -sin], [sin, cos]])
    forward = np.block([[cos, sin], [-sin, cos]])
    place = np.zeros((PW, ROWS), np.int64) - 1
    for d in range(PW):
        for ri in range(2):
            for zi in range(DEPTH):
                place[d, ri * DEPTH + zi] = ri * GRID + d * DEPTH + zi
    flat = place.reshape(-1)
    to_planes = np.where((flat >= 0)[:, None], inverse[np.maximum(flat, 0)], 0.0)
    from_planes = np.where((flat >= 0)[None, :], forward[:, np.maximum(flat, 0)], 0.0)
    used = BANDS * 2 * DEPTH
    spread = np.zeros((8, 2 * LANES, 2 * LANES))
    for s in range(8):
        for b in range(BANDS):
            for r in range(2 * DEPTH):
                for g in range(GROUPS):
                    spread[s, b * LANES + s * ROWS + r, g * WIDTH + b * 2 * DEPTH + r] = 1.0
        spread[s, s * ROWS + 2 * DEPTH, LANES:] = 1.0
    turn = np.zeros((LANES, LANES))
    fold = np.zeros((2 * ROWS, LANES))
    for g in range(GROUPS):
        for b in range(BANDS):
            for zi in range(DEPTH):
                re = g * WIDTH + b * 2 * DEPTH + zi
                im = re + DEPTH
                turn[re, im] = -1.0
                turn[im, re] = 1.0
                fold[b * ROWS + zi, re] = 1.0
                fold[b * ROWS + DEPTH + zi, im] = 1.0
    unit = np.eye(LANES)
    return dict(
        to_planes=to_planes,
        from_planes=from_planes,
        spread=spread,
        y_table=np.concatenate([cos, sin], axis=0),
        mix_in=np.concatenate([unit, turn], axis=1),
        mix_out=np.concatenate([unit, turn], axis=0),
        x_inverse=inverse,
        x_forward=forward,
        fold=fold,
    )


def dot(a, b, precision=None):
    return lax.dot_general(
        a, b, (((1,), (0,)), ((), ())), precision=precision, preferred_element_type=F32
    )


def dot_nt(a, b, precision=None):
    return lax.dot_general(
        a, b, (((1,), (1,)), ((), ())), precision=precision, preferred_element_type=F32
    )


def wrapped(freqs):
    return jnp.where(freqs >= GRID // 2, freqs - GRID, freqs)


def send_kernel(block_ref, beta_ref, columns_ref, table_ref, send_ref):
    sums = []
    for b in range(BANDS):
        for j in range(PROJ):
            br, bi = beta_ref[j, 0], beta_ref[j, 1]
            wr, wi = block_ref[b, 0], block_ref[b, 1]
            sums.append(jnp.sum(br * wr + bi * wi, axis=0, keepdims=True))
            sums.append(jnp.sum(br * wi - bi * wr, axis=0, keepdims=True))
    stacked = jnp.concatenate(sums, axis=0)
    spread = jnp.concatenate([stacked, jnp.zeros((LANES - 32, LANES), F32)], axis=0)
    total = dot_nt(jnp.ones((8, LANES), F32), spread, HIGHEST)[0:1]
    high = total.astype(BF).astype(F32)
    middle = (total - high).astype(BF).astype(F32)
    low = total - high - middle
    cols = columns_ref[...]
    col_x = cols // GRID
    first = jnp.concatenate([col_x, cols - col_x * GRID], axis=1).astype(F32)
    other = jnp.concatenate([high, middle, low], axis=0)
    other = jnp.concatenate([other, jnp.zeros((3, LANES), F32)], axis=1)
    meta = jnp.concatenate([jnp.zeros((2 * DEPTH, 2 * LANES), F32), first, other], axis=0)
    wave = jnp.concatenate(
        [jnp.concatenate([block_ref[b, 0], block_ref[b, 1]], axis=0) for b in range(BANDS)], axis=1
    )
    lines = dot(table_ref[...], wave, HIGHEST)
    lines = lines.reshape(PW, ROWS, 2 * LANES) + meta[None]
    send_ref[...] = lines.astype(BF)


def planes_kernel(
    index_ref,
    recv_ref,
    pot_ref,
    spread_ref,
    y_ref,
    mix_in_ref,
    mix_out_ref,
    x_inv_ref,
    x_fwd_ref,
    fold_ref,
    back_ref,
    rows_ref,
    mask_ref,
    grid_ref,
    near_ref,
    far_ref,
):
    lane_group = lax.broadcasted_iota(jnp.int32, (1, LANES), 1) // WIDTH
    group_start = (lane_group * SPAN).astype(F32)
    turned = recv_ref[...].astype(F32).T.astype(BF)
    for s in range(8):
        for g in range(PW // 8):
            left = jnp.concatenate(
                [
                    turned[0:LANES, g * LANES : (g + 1) * LANES],
                    turned[LANES : 2 * LANES, g * LANES : (g + 1) * LANES],
                ],
                axis=1,
            )
            both = dot(left, spread_ref[s])
            start = (g * 8 + s) * LANES
            rows_ref[start : start + LANES, :] = both[:, :LANES]
            offset = both[:, LANES:] - group_start
            mask_ref[start : start + LANES, :] = jnp.where(
                (offset >= 0.0) & (offset < SPAN), 1.0, 0.0
            )

    def clear(i, _):
        grid_ref[pl.ds(pl.multiple_of(i * 256, 256), 256), :] = jnp.zeros((256, LANES), F32)
        return 0

    lax.fori_loop(0, SPAN * GRID // 256, clear, 0)

    def scatter(i, _):
        base = pl.multiple_of(i * 16, 16)
        for u in range(16):
            code = index_ref[base + u]
            row = rows_ref[pl.ds(base + u, 1), :]
            pltpu.store(
                grid_ref.at[pl.ds(code >> 2, 1), :], row, mask=lane_group == (code & 3)
            )
        return 0

    lax.fori_loop(0, COLS // 16, scatter, 0)

    def along_y_in(i, _):
        base = pl.multiple_of(i * 2 * GRID, 2 * GRID)
        pair = jnp.concatenate(
            [grid_ref[pl.ds(base, GRID), :], grid_ref[pl.ds(base + GRID, GRID), :]], axis=1
        ).astype(BF)
        both = dot(y_ref[...], pair).astype(BF)
        for h in range(2):
            part = jnp.concatenate(
                [
                    both[:GRID, h * LANES : (h + 1) * LANES],
                    both[GRID:, h * LANES : (h + 1) * LANES],
                ],
                axis=1,
            )
            mixed = dot_nt(mix_in_ref[...], part)
            place = pl.ds(pl.multiple_of((2 * i + h) * LANES, LANES), LANES)
            near_ref[place, :] = mixed[:, :LANES]
            far_ref[place, :] = jnp.concatenate(
                [mixed[:, LANES:], jnp.zeros((LANES, 2 * LANES - GRID), F32)], axis=1
            )
        return 0

    lax.fori_loop(0, SPAN // 2, along_y_in, 0)

    for b in range(BANDS):
        for zi in range(DEPTH):
            lane = b * 2 * DEPTH + zi
            places = [
                pl.ds(g * WIDTH + lane + ri * DEPTH, SPAN, stride=LANES)
                for ri in range(2)
                for g in range(GROUPS)
            ]
            plane = jnp.concatenate(
                [
                    jnp.concatenate([ref[place, :] for place in places], axis=0)
                    for ref in (near_ref, far_ref)
                ],
                axis=1,
            ).astype(BF)
            field = dot(x_inv_ref[...], plane)
            pot = jnp.concatenate(
                [pot_ref[zi], jnp.zeros((GRID, 2 * LANES - GRID), F32)], axis=1
            )
            field = (field * jnp.concatenate([pot, pot], axis=0)).astype(BF)
            back = dot(x_fwd_ref[...], field)
            for k, place in enumerate(places):
                near_ref[place, :] = back[k * SPAN : (k + 1) * SPAN, :LANES]
                far_ref[place, :] = back[k * SPAN : (k + 1) * SPAN, LANES:]

    def along_y_out(i, _):
        place = pl.ds(pl.multiple_of(i * 2 * LANES, 2 * LANES), 2 * LANES)
        pair = jnp.concatenate(
            [near_ref[place, :], far_ref[place, : GRID - LANES]], axis=1
        ).astype(BF)
        both = dot_nt(y_ref[...], pair).astype(BF)
        base = pl.multiple_of(i * 2 * GRID, 2 * GRID)
        for h in range(2):
            part = jnp.concatenate(
                [
                    both[:GRID, h * LANES : (h + 1) * LANES],
                    both[GRID:, h * LANES : (h + 1) * LANES],
                ],
                axis=1,
            )
            grid_ref[pl.ds(base + h * GRID, GRID), :] = dot(part, mix_out_ref[...])
        return 0

    lax.fori_loop(0, SPAN // 2, along_y_out, 0)

    def gather(i, _):
        base = pl.multiple_of(i * 16, 16)
        for u in range(16):
            code = index_ref[base + u]
            rows_ref[pl.ds(base + u, 1), :] = grid_ref[pl.ds(code >> 2, 1), :]
        return 0

    lax.fori_loop(0, COLS // 16, gather, 0)

    for d in range(PW):
        part = slice(d * LANES, (d + 1) * LANES)
        kept = (rows_ref[part, :] * mask_ref[part, :]).astype(BF)
        folded = dot_nt(fold_ref[...], kept).astype(BF)
        back_ref[d * ROWS : (d + 1) * ROWS, 0:LANES] = folded[:ROWS]
        back_ref[d * ROWS : (d + 1) * ROWS, LANES:] = folded[ROWS:]


def finish_kernel(
    mixed_ref, back_ref, block_ref, beta_ref, columns_ref, table_ref, *rest
):
    others = rest[:4]
    applied_ref, cross_ref, local_ref = rest[4:]
    local_ref[...] = dot(table_ref[0], back_ref[...]) + dot(table_ref[1], back_ref[...])
    cols = columns_ref[...]
    col_x = cols // GRID
    fx = wrapped(col_x)
    fy = wrapped(cols - col_x * GRID)
    fxy = fx * fx + fy * fy
    chunk = 48
    totals = [jnp.zeros((8, LANES), F32) for _ in range(32)]
    for start in range(0, GRID, chunk):
        part = slice(start, start + chunk)
        fz = wrapped(lax.broadcasted_iota(jnp.int32, (chunk, LANES), 0) + start)
        kinetic = (fz * fz + fxy).astype(F32) * (4.0 / (GRID * GRID))
        low = []
        for b in range(BANDS):
            real = local_ref[start : start + chunk, b * LANES : (b + 1) * LANES]
            imag = local_ref[GRID + start : GRID + start + chunk, b * LANES : (b + 1) * LANES]
            real = real + kinetic * block_ref[b, 0, part]
            imag = imag + kinetic * block_ref[b, 1, part]
            for k in range(PROJ):
                mr = mixed_ref[b * 2 * PROJ + 2 * k]
                mi = mixed_ref[b * 2 * PROJ + 2 * k + 1]
                br, bi = beta_ref[k, 0, part], beta_ref[k, 1, part]
                real = real + mr * br - mi * bi
                imag = imag + mr * bi + mi * br
            applied_ref[b, 0, part] = real
            applied_ref[b, 1, part] = imag
            low.append((real.astype(BF).astype(F32), imag.astype(BF).astype(F32)))
        for o in range(4):
            for m in range(BANDS):
                otr = others[o][m, 0, part].astype(F32)
                oti = others[o][m, 1, part].astype(F32)
                for n in range(BANDS):
                    ar, ai = low[n]
                    real = (otr * ar + oti * ai).reshape(chunk // 8, 8, LANES).sum(0)
                    imag = (otr * ai - oti * ar).reshape(chunk // 8, 8, LANES).sum(0)
                    totals[o * 8 + m * 2 + n] += real
                    totals[o * 8 + 4 + m * 2 + n] += imag
    stacked = jnp.concatenate([jnp.sum(t, axis=0, keepdims=True) for t in totals], axis=0)
    spread = jnp.concatenate([stacked, jnp.zeros((LANES - 32, LANES), F32)], axis=0)
    cross_ref[...] = dot_nt(jnp.ones((8, LANES), F32), spread, HIGHEST)


def from_behind(value, axis, steps):
    count = lax.axis_size(axis)
    first, last = max(0, -steps), min(count, count - steps)
    return lax.ppermute(value, axis, [(s, s + steps) for s in range(first, last)])


def vmem():
    return pl.BlockSpec(memory_space=pltpu.VMEM)


def smem():
    return pl.BlockSpec(memory_space=pltpu.SMEM)


def exchange(value):
    return lax.all_to_all(value, "pw", split_axis=0, concat_axis=0, tiled=True)


def per_device(orbitals, potential, projectors, coupling, columns):
    tables = build_tables()
    half = {k: jnp.asarray(v, BF) for k, v in tables.items()}
    block = orbitals[0]
    own_columns = columns.reshape(1, LOCAL)
    scale = 1.0 / math.sqrt(COLS * GRID)
    low_orbitals = block.astype(BF)
    others = [from_behind(low_orbitals, "band", -offset) for offset in (-2, -1, 1, 2)]

    sent = pl.pallas_call(
        send_kernel,
        name="lines_out",
        out_shape=jax.ShapeDtypeStruct((PW, ROWS, 2 * LANES), BF),
        in_specs=[vmem()] * 4,
        out_specs=vmem(),
        compiler_params=pltpu.CompilerParams(vmem_limit_bytes=32 << 20),
    )(block, projectors, own_columns, jnp.asarray(tables["to_planes"], F32))
    recv = exchange(sent)

    all_x = recv[:, 2 * DEPTH, :LOCAL].astype(jnp.int32)
    all_y = recv[:, 2 * DEPTH, LOCAL:].astype(jnp.int32)
    index = (((all_x % SPAN) * GRID + all_y) * GROUPS + all_x // SPAN).reshape(COLS)
    proj = jnp.sum(recv[:, 2 * DEPTH + 1 :, :32].astype(F32), axis=(0, 1))
    proj = proj.reshape(BANDS, PROJ, 2) * scale
    coupling_sym = 0.5 * (coupling + coupling.T)
    mixed = jnp.sum(proj[:, :, None, :] * coupling_sym[None, :, :, None], axis=1)
    mixed = mixed.reshape(BANDS * PROJ * 2)

    back = pl.pallas_call(
        planes_kernel,
        name="planes",
        out_shape=jax.ShapeDtypeStruct((PW * ROWS, 2 * LANES), BF),
        in_specs=[smem()] + [vmem()] * 9,
        out_specs=vmem(),
        scratch_shapes=[
            pltpu.VMEM((COLS, LANES), F32),
            pltpu.VMEM((COLS, LANES), F32),
            pltpu.VMEM((SPAN * GRID, LANES), F32),
            pltpu.VMEM((SPAN * LANES, LANES), F32),
            pltpu.VMEM((SPAN * LANES, LANES), F32),
        ],
        compiler_params=pltpu.CompilerParams(vmem_limit_bytes=48 << 20),
    )(
        index,
        recv.reshape(PW * ROWS, 2 * LANES),
        potential,
        half["spread"],
        half["y_table"],
        half["mix_in"],
        half["mix_out"],
        half["x_inverse"],
        half["x_forward"],
        half["fold"],
    )
    returned = exchange(back.reshape(PW, ROWS, 2 * LANES)).reshape(PW * ROWS, 2 * LANES)

    exact = tables["from_planes"]
    rounded = exact.astype(jnp.bfloat16).astype(np.float64)
    pair = jnp.asarray(np.stack([rounded, exact - rounded]), BF)
    applied, cross = pl.pallas_call(
        finish_kernel,
        name="lines_in",
        out_shape=(
            jax.ShapeDtypeStruct((BANDS, 2, GRID, LOCAL), F32),
            jax.ShapeDtypeStruct((8, LANES), F32),
        ),
        in_specs=[smem()] + [vmem()] * 9,
        out_specs=(vmem(), vmem()),
        scratch_shapes=[pltpu.VMEM((2 * GRID, 2 * LANES), F32)],
        compiler_params=pltpu.CompilerParams(vmem_limit_bytes=32 << 20),
    )(mixed, returned, block, projectors, own_columns, pair, *others)
    every = exchange(jnp.broadcast_to(cross[0:1], (PW, LANES)))
    summed = jnp.sum(every[:, :32], axis=0).reshape(4, 2, BANDS, BANDS)
    return applied[None], (summed * scale)[None]


def solution(mesh):
    return jax.shard_map(
        per_device,
        mesh=mesh,
        in_specs=(
            P("band", None, None, None, "pw"),
            P("pw", None, None),
            P(None, None, None, "pw"),
            P(),
            P("pw"),
        ),
        out_specs=(P("band", None, None, None, "pw"), P("band", None, None, None, None)),
        check_vma=False,
    )
```

time: 639 us -> 125 us (0.20)
  the two profiles are of different devices: /device:TPU:132 before, /device:TPU:3 now
where the time goes in v1:
time: 125 us; the launch traced here: 124 us
  Pallas kernels  50.3 us (40%)
  starting transfers between devices  37 us (30%)
  local copies, waits for them, and re-layouts  13.6 us (11%)
  blocking collectives  10.9 us (9%)
  waiting for transfers between devices  9.87 us (8%)
  other arithmetic  1.81 us (1%)
    pallas_call x1, Pallas kernels, per_device(): pl.pallas_call(planes_kernel, name='planes', out_shape=jax.ShapeDtypeStru...  45 us
    ppermute x4, starting transfers between devices, from_behind(): lax.ppermute(value, axis, [(s, s + steps) for s in range(first, last)])  18.8 us
    all_to_all x2, starting transfers between devices, exchange(): return lax.all_to_all(value, 'pw', split_axis=0, concat_axis=0, tiled=True)  18.2 us
    unnamed x42, local copies, waits for them, and re-layouts  13.2 us
    all_to_all x1, blocking collectives, exchange(): return lax.all_to_all(value, 'pw', split_axis=0, concat_axis=0, tiled=True)  10.9 us
    all_to_all x2, waiting for transfers between devices, exchange(): return lax.all_to_all(value, 'pw', split_axis=0, concat_axis=0, tiled=True)  9.86 us
    pallas_call x1, Pallas kernels, per_device(): pl.pallas_call(finish_kernel, name='lines_in', out_shape=(jax.ShapeDtypeS...  3.05 us
  transfers between devices with their start and end apart: 6, of which 1 were waited for; matrix products, arithmetic and copies ran while one was open for 2% of the time, Pallas kernels for 36%

profile of v1, /device:TPU:3, one launch (start us, length us, event | category | flops | bytes accessed | tf_op | source)
XLA Modules:
  0.0 124.4 jit_solution(1998617501607638824)
XLA Ops:
  0.6 1.4 %copy-done = f32[8,2,192,128]{3,2,1,0:T(8,128)S(1)} copy-done((f32[8,2,192,128]{3,2,1,0:T(8,128)S(1)}, f32[8,2,192,128]{3,2,1,0:T(8,128)}, u32[]{:S(2)}) %copy-start) | copy-done | bytes 1572888
  2.0 1.0 copy-done.2
  3.0 1.1 copy-done.10
  4.2 0.7 copy-done.17
  4.9 2.3 %lines_out.1 = bf16[32,16,256]{2,1,0:T(8,128)(2,1)} custom-call(f32[2,2,192,128]{3,2,1,0:T(8,128)S(1)} %bitcast.21, f32[8,2,192,128]{3,2,1,0:T(8,128)S(1)} %copy-done, s32[1,128]{1,0:T(1,128)S(1)} %bitcast.26, f32[512,384]{1,0:T(8,128)S(1)} %copy-done.10), custom_call_target="tpu_custom_call" | custom-call | tf_op jit(solution)/shard_map/lines_out/pallas_call | solution.py:341
  7.2 9.4 %all-to-all-start = ((bf16[32,16,256]{2,1,0:T(8,128)(2,1)}), bf16[32,16,256]{2,1,0:T(8,128)(2,1)S(1)}, u32[]{:S(2)}, u32[]{:S(2)}) async-start(bf16[32,16,256]{2,1,0:T(8,128)(2,1)} %lines_out.1), calls=%async_computation | async-start | bytes 524288 | tf_op jit(solution)/shard_map/all_to_all | solution.py:329
  16.5 0.7 bitcast_convert_fusion
  17.2 1.3 %collective-permute-start.3 = (bf16[2,2,192,128]{3,2,1,0:T(8,128)(2,1)}, bf16[2,2,192,128]{3,2,1,0:T(8,128)(2,1)}, u32[]{:S(2)}, u32[]{:S(2)}) collective-permute-start(bf16[2,2,192,128]{3,2,1,0:T(8,128)(2,1)} %bitcast_convert_fusion), channel_id=1, source_target_pairs={{64,0},{96,32},{128,64},{160,96},{192,128},{224,160},{65,1},{97,33... | collective-permute-start | bytes 589832 | tf_op jit(solution)/shard_map/ppermute | solution.py:317
  18.5 2.2 %collective-permute-start.2 = (bf16[2,2,192,128]{3,2,1,0:T(8,128)(2,1)}, bf16[2,2,192,128]{3,2,1,0:T(8,128)(2,1)}, u32[]{:S(2)}, u32[]{:S(2)}) collective-permute-start(bf16[2,2,192,128]{3,2,1,0:T(8,128)(2,1)} %bitcast_convert_fusion), channel_id=1, source_target_pairs={{32,0},{64,32},{96,64},{128,96},{160,128},{192,160},{224,192},{33,... | collective-permute-start | bytes 589832 | tf_op jit(solution)/shard_map/ppermute | solution.py:317
  20.7 3.7 %collective-permute-start.1 = (bf16[2,2,192,128]{3,2,1,0:T(8,128)(2,1)}, bf16[2,2,192,128]{3,2,1,0:T(8,128)(2,1)}, u32[]{:S(2)}, u32[]{:S(2)}) collective-permute-start(bf16[2,2,192,128]{3,2,1,0:T(8,128)(2,1)} %bitcast_convert_fusion), channel_id=1, source_target_pairs={{0,32},{32,64},{64,96},{96,128},{128,160},{160,192},{192,224},{1,3... | collective-permute-start | bytes 589832 | tf_op jit(solution)/shard_map/ppermute | solution.py:317
  24.4 11.6 %collective-permute-start = (bf16[2,2,192,128]{3,2,1,0:T(8,128)(2,1)}, bf16[2,2,192,128]{3,2,1,0:T(8,128)(2,1)}, u32[]{:S(2)}, u32[]{:S(2)}) collective-permute-start(bf16[2,2,192,128]{3,2,1,0:T(8,128)(2,1)} %bitcast_convert_fusion), channel_id=1, source_target_pairs={{0,64},{32,96},{64,128},{96,160},{128,192},{160,224},{1,65},{33,97... | collective-permute-start | bytes 589832 | tf_op jit(solution)/shard_map/ppermute | solution.py:317
  36.0 0.7 copy.25
  36.7 0.1 compare_reduce_fusion
  37.0 1.2 copy-done.6
  38.2 1.0 copy-done.11
  39.2 1.0 copy-done.12
  40.1 0.9 copy-done.13
  41.1 45.0 %planes.1 = bf16[512,256]{1,0:T(8,128)(2,1)S(1)} custom-call(s32[4096]{0:T(1024)S(1)} %fusion.3.index_ref, bf16[512,256]{1,0:T(8,128)(2,1)S(1)} %bitcast.23, f32[6,192,192]{2,1,0:T(8,128)S(1)} %copy-done.4, bf16[8,256,256]{2,1,0:T(8,128)(2,1)S(1)} %copy-done.6, bf16[384,192]{1,0:T(8,128)(2,1)S(1)} %copy-done.13, bf16[128,256]{1,0:T(8,128)(2,1)S(1)} %copy-done.15, ...), custom_call_target="tpu_custom_call" | custom-call | tf_op jit(solution)/shard_map/planes/pallas_call | solution.py:360
  86.1 0.7 copy-done.5
  86.8 8.8 %all-to-all-start.1 = ((bf16[32,16,256]{2,1,0:T(8,128)(2,1)}), bf16[32,16,256]{2,1,0:T(8,128)(2,1)S(1)}, u32[]{:S(2)}, u32[]{:S(2)}) async-start(bf16[32,16,256]{2,1,0:T(8,128)(2,1)} %bitcast.24), calls=%async_computation.1 | async-start | bytes 524288 | tf_op jit(solution)/shard_map/all_to_all | solution.py:329
  95.6 0.7 fusion.4
  96.5 0.1 copy.24
  96.6 0.1 multiply_reduce_fusion
  96.7 0.1 reshape.61.mixed_ref
  96.9 9.9 %all-to-all-done.1 = bf16[32,16,256]{2,1,0:T(8,128)(2,1)S(1)} async-done(((bf16[32,16,256]{2,1,0:T(8,128)(2,1)}), bf16[32,16,256]{2,1,0:T(8,128)(2,1)S(1)}, u32[]{:S(2)}, u32[]{:S(2)}) %all-to-all-start.1) | async-done | bytes 262176 | tf_op jit(solution)/shard_map/all_to_all | solution.py:329
  106.7 0.7 copy-done.7
  107.5 0.9 copy-done.8
  108.4 1.1 copy-done.9
  109.5 3.0 %lines_in.1 = (f32[2,2,192,128]{3,2,1,0:T(8,128)}, f32[8,128]{1,0:T(8,128)S(1)}) custom-call(f32[32]{0:T(128)S(1)} %reshape.61.mixed_ref, bf16[512,256]{1,0:T(8,128)(2,1)S(1)} %bitcast.25, f32[2,2,192,128]{3,2,1,0:T(8,128)S(1)} %bitcast.22, f32[8,2,192,128]{3,2,1,0:T(8,128)S(1)} %copy-done.1, s32[1,128]{1,0:T(1,128)S(1)} %bitcast.27, ...), custom_call_target="tpu_custom_call" | custom-call | tf_op jit(solution)/shard_map/lines_in/pallas_call | solution.py:391
  112.6 10.9 %all_to_all.19 = f32[32,1,128]{2,1,0:T(1,128)S(1)} all-to-all(f32[32,1,128]{2,1,0:T(1,128)S(1)} %broadcast_in_dim.5), channel_id=1, replica_groups=mesh['band'=8,'pw'=32] {'pw'}, dimensions={0} | all-to-all | bytes 32768 | tf_op jit(solution)/shard_map/all_to_all | solution.py:329
  123.6 0.1 mul.73
  123.7 0.7 copy.27
  (44 shorter events, 0.5 us)
Async XLA Ops:
  0.6 1.4 %copy-start = (f32[8,2,192,128]{3,2,1,0:T(8,128)S(1)}, f32[8,2,192,128]{3,2,1,0:T(8,128)}, u32[]{:S(2)}) copy-start(f32[8,2,192,128]{3,2,1,0:T(8,128)} %beta_ref.3) | copy-start | bytes 4718596
  2.0 1.0 copy-start.2
  3.0 1.1 copy-start.10
  4.2 0.7 copy-start.17
  4.8 11.7 %copy-start.3 = (f32[1,2,2,192,128]{4,3,2,1,0:T(8,128)S(1)}, f32[1,2,2,192,128]{4,3,2,1,0:T(8,128)}, u32[]{:S(2)}) copy-start(f32[1,2,2,192,128]{4,3,2,1,0:T(8,128)} %param.14) | copy-start | bytes 1179652
  4.8 31.2 %copy-start.19 = (f32[8,8]{1,0:T(8,128)S(1)}, f32[8,8]{1,0:T(8,128)}, u32[]{:S(2)}) copy-start(f32[8,8]{1,0:T(8,128)} %param.17) | copy-start | bytes 772
  4.8 32.1 %copy-start.4 = (f32[6,192,192]{2,1,0:T(8,128)S(1)}, f32[6,192,192]{2,1,0:T(8,128)}, u32[]{:S(2)}) copy-start(f32[6,192,192]{2,1,0:T(8,128)} %pot_ref.1) | copy-start | bytes 2654212
  4.8 32.1 %copy-start.14 = (bf16[256,128]{1,0:T(8,128)(2,1)S(1)}, bf16[256,128]{1,0:T(8,128)(2,1)}, u32[]{:S(2)}) copy-start(bf16[256,128]{1,0:T(8,128)(2,1)} %constant.52.clone.mix_out_ref) | copy-start | bytes 196612
  4.8 32.1 %copy-start.15 = (bf16[128,256]{1,0:T(8,128)(2,1)S(1)}, bf16[128,256]{1,0:T(8,128)(2,1)}, u32[]{:S(2)}) copy-start(bf16[128,256]{1,0:T(8,128)(2,1)} %constant.51.clone.mix_in_ref) | copy-start | bytes 196612
  4.9 32.1 %copy-start.16 = (bf16[32,128]{1,0:T(8,128)(2,1)S(1)}, bf16[32,128]{1,0:T(8,128)(2,1)}, u32[]{:S(2)}) copy-start(bf16[32,128]{1,0:T(8,128)(2,1)} %constant.55.clone.fold_ref) | copy-start | bytes 24580
  7.2 29.5 %all-to-all-start = ((bf16[32,16,256]{2,1,0:T(8,128)(2,1)}), bf16[32,16,256]{2,1,0:T(8,128)(2,1)S(1)}, u32[]{:S(2)}, u32[]{:S(2)}) async-start(bf16[32,16,256]{2,1,0:T(8,128)(2,1)} %lines_out.1), calls=%async_computation | async-start | bytes 524288 | tf_op jit(solution)/shard_map/all_to_all | solution.py:329
  17.2 79.6 %collective-permute-start.3 = (bf16[2,2,192,128]{3,2,1,0:T(8,128)(2,1)}, bf16[2,2,192,128]{3,2,1,0:T(8,128)(2,1)}, u32[]{:S(2)}, u32[]{:S(2)}) collective-permute-start(bf16[2,2,192,128]{3,2,1,0:T(8,128)(2,1)} %bitcast_convert_fusion), channel_id=1, source_target_pairs={{64,0},{96,32},{128,64},{160,96},{192,128},{224,160},{65,1},{97,33... | collective-permute-start | bytes 589832 | tf_op jit(solution)/shard_map/ppermute | solution.py:317
  18.5 78.3 %collective-permute-start.2 = (bf16[2,2,192,128]{3,2,1,0:T(8,128)(2,1)}, bf16[2,2,192,128]{3,2,1,0:T(8,128)(2,1)}, u32[]{:S(2)}, u32[]{:S(2)}) collective-permute-start(bf16[2,2,192,128]{3,2,1,0:T(8,128)(2,1)} %bitcast_convert_fusion), channel_id=1, source_target_pairs={{32,0},{64,32},{96,64},{128,96},{160,128},{192,160},{224,192},{33,... | collective-permute-start | bytes 589832 | tf_op jit(solution)/shard_map/ppermute | solution.py:317
  20.7 76.2 %collective-permute-start.1 = (bf16[2,2,192,128]{3,2,1,0:T(8,128)(2,1)}, bf16[2,2,192,128]{3,2,1,0:T(8,128)(2,1)}, u32[]{:S(2)}, u32[]{:S(2)}) collective-permute-start(bf16[2,2,192,128]{3,2,1,0:T(8,128)(2,1)} %bitcast_convert_fusion), channel_id=1, source_target_pairs={{0,32},{32,64},{64,96},{96,128},{128,160},{160,192},{192,224},{1,3... | collective-permute-start | bytes 589832 | tf_op jit(solution)/shard_map/ppermute | solution.py:317
  24.4 72.4 %collective-permute-start = (bf16[2,2,192,128]{3,2,1,0:T(8,128)(2,1)}, bf16[2,2,192,128]{3,2,1,0:T(8,128)(2,1)}, u32[]{:S(2)}, u32[]{:S(2)}) collective-permute-start(bf16[2,2,192,128]{3,2,1,0:T(8,128)(2,1)} %bitcast_convert_fusion), channel_id=1, source_target_pairs={{0,64},{32,96},{64,128},{96,160},{128,192},{160,224},{1,65},{33,97... | collective-permute-start | bytes 589832 | tf_op jit(solution)/shard_map/ppermute | solution.py:317
  37.0 1.2 copy-start.6
  38.2 1.0 copy-start.11
  39.2 1.0 copy-start.12
  40.1 0.9 copy-start.13
  41.1 66.4 %copy-start.1 = (f32[8,2,192,128]{3,2,1,0:T(8,128)S(1)}, f32[8,2,192,128]{3,2,1,0:T(8,128)}, u32[]{:S(2)}) copy-start(f32[8,2,192,128]{3,2,1,0:T(8,128)} %beta_ref.3) | copy-start | bytes 4718596
  41.1 66.4 %copy-start.18 = (s32[128]{0:T(128)S(1)}, s32[128]{0:T(128)}, u32[]{:S(2)}) copy-start(s32[128]{0:T(128)} %param.18) | copy-start | bytes 1540
  86.1 0.7 copy-start.5
  86.8 20.0 %all-to-all-start.1 = ((bf16[32,16,256]{2,1,0:T(8,128)(2,1)}), bf16[32,16,256]{2,1,0:T(8,128)(2,1)S(1)}, u32[]{:S(2)}, u32[]{:S(2)}) async-start(bf16[32,16,256]{2,1,0:T(8,128)(2,1)} %bitcast.24), calls=%async_computation.1 | async-start | bytes 524288 | tf_op jit(solution)/shard_map/all_to_all | solution.py:329
  106.7 0.7 copy-start.7
  107.5 1.0 copy-start.8
  108.4 1.1 copy-start.9

commit v2 on v1

v2 whole, which is shorter than its diff:
```python
from functools import partial
import math

import jax
import jax.numpy as jnp
import numpy as np
from jax import lax
from jax.experimental import pallas as pl
from jax.experimental.pallas import tpu as pltpu
from jax.sharding import PartitionSpec as P

GRID = 192
BANDS = 2
PROJ = 8
PW = 32
LOCAL = 128
COLS = PW * LOCAL
DEPTH = GRID // PW
ROWS = 16
GROUPS = 4
SPAN = GRID // GROUPS
LANES = 128
WIDTH = LANES // GROUPS
STEP = LANES + 1
BF = jnp.bfloat16
F32 = jnp.float32
HIGHEST = lax.Precision.HIGHEST


def dft_tables():
    index = np.arange(GRID)
    angle = (index[:, None] * index[None, :] % GRID) * (2.0 * math.pi / GRID)
    factor = 1.0 / math.sqrt(GRID)
    return np.cos(angle) * factor, np.sin(angle) * factor


def build_tables():
    cos, sin = dft_tables()
    inverse = np.block([[cos, -sin], [sin, cos]])
    forward = np.block([[cos, sin], [-sin, cos]])
    place = np.zeros((PW, ROWS), np.int64) - 1
    for d in range(PW):
        for ri in range(2):
            for zi in range(DEPTH):
                place[d, ri * DEPTH + zi] = ri * GRID + d * DEPTH + zi
    flat = place.reshape(-1)
    to_planes = np.where((flat >= 0)[:, None], inverse[np.maximum(flat, 0)], 0.0)
    from_planes = np.where((flat >= 0)[None, :], forward[:, np.maximum(flat, 0)], 0.0)
    used = BANDS * 2 * DEPTH
    spread = np.zeros((8, 2 * LANES, 2 * LANES))
    for s in range(8):
        for b in range(BANDS):
            for r in range(2 * DEPTH):
                for g in range(GROUPS):
                    spread[s, b * LANES + s * ROWS + r, g * WIDTH + b * 2 * DEPTH + r] = 1.0
        spread[s, s * ROWS + 2 * DEPTH, LANES:] = 1.0
    mix_in = np.zeros((LANES, 2 * LANES))
    mix_out = np.zeros((2 * LANES, LANES))
    fold = np.zeros((2 * ROWS, LANES))
    for g in range(GROUPS):
        for b in range(BANDS):
            for zi in range(DEPTH):
                re = g * WIDTH + b * 2 * DEPTH + zi
                im = re + DEPTH
                for h in range(GROUPS):
                    other = h * WIDTH + b * 2 * DEPTH + zi
                    for part, factor in ((0, 1.0), (LANES, 1j)):
                        turn = 1j ** (g * h % 4) * factor
                        mix_in[re, part + other] = turn.real
                        mix_in[re, part + other + DEPTH] = -turn.imag
                        mix_in[im, part + other] = turn.imag
                        mix_in[im, part + other + DEPTH] = turn.real
                        turn = turn.conjugate()
                        mix_out[part + other, re] = turn.real
                        mix_out[part + other + DEPTH, re] = -turn.imag
                        mix_out[part + other, im] = turn.imag
                        mix_out[part + other + DEPTH, im] = turn.real
                fold[b * ROWS + zi, re] = 1.0
                fold[b * ROWS + DEPTH + zi, im] = 1.0
    x_inverse = np.zeros((GROUPS, 2 * SPAN, 2 * SPAN))
    x_forward = np.zeros((GROUPS, 2 * SPAN, 2 * SPAN))
    for g in range(GROUPS):
        c, s = cos[:SPAN, g::GROUPS], sin[:SPAN, g::GROUPS]
        x_inverse[g] = np.block([[c.T, -s.T], [s.T, c.T]])
        x_forward[g] = np.block([[c, s], [-s, c]])
    return dict(
        to_planes=to_planes,
        from_planes=from_planes,
        spread=spread,
        y_table=np.concatenate([cos, sin], axis=0),
        mix_in=mix_in,
        mix_out=mix_out,
        x_inverse=x_inverse,
        x_forward=x_forward,
        fold=fold,
    )


def dot(a, b, precision=None):
    return lax.dot_general(
        a, b, (((1,), (0,)), ((), ())), precision=precision, preferred_element_type=F32
    )


def dot_nt(a, b, precision=None):
    return lax.dot_general(
        a, b, (((1,), (1,)), ((), ())), precision=precision, preferred_element_type=F32
    )


def wrapped(freqs):
    return jnp.where(freqs >= GRID // 2, freqs - GRID, freqs)


def load(source, target, sem):
    copy = pltpu.make_async_copy(source, target, sem)
    copy.start()
    return copy


def send_kernel(
    block_hbm,
    beta_hbm,
    columns_ref,
    table_hbm,
    send_hbm,
    low_hbm,
    block_ref,
    beta_ref,
    table_ref,
    lines_ref,
    low_ref,
    sems,
):
    block_copy = load(block_hbm, block_ref, sems.at[0])
    table_copy = load(table_hbm, table_ref, sems.at[1])
    beta_copies = [load(beta_hbm.at[j], beta_ref.at[j], sems.at[2 + j]) for j in range(PROJ)]
    block_copy.wait()
    low_ref[...] = block_ref[...].astype(BF)
    low_copy = load(low_ref, low_hbm, sems.at[11])
    wave = jnp.concatenate(
        [jnp.concatenate([block_ref[b, 0], block_ref[b, 1]], axis=0) for b in range(BANDS)], axis=1
    )
    wave_high = wave.astype(BF)
    wave_low = (wave - wave_high.astype(F32)).astype(BF)
    table_copy.wait()
    lines = dot(table_ref[0], wave_high) + (dot(table_ref[1], wave_high) + dot(table_ref[0], wave_low))
    sums = [None] * (BANDS * PROJ * 2)
    for j in range(PROJ):
        beta_copies[j].wait()
        for b in range(BANDS):
            br, bi = beta_ref[j, 0], beta_ref[j, 1]
            wr, wi = block_ref[b, 0], block_ref[b, 1]
            at = (b * PROJ + j) * 2
            sums[at] = jnp.sum(br * wr + bi * wi, axis=0, keepdims=True)
            sums[at + 1] = jnp.sum(br * wi - bi * wr, axis=0, keepdims=True)
    stacked = jnp.concatenate(sums, axis=0)
    spread = jnp.concatenate([stacked, jnp.zeros((LANES - 32, LANES), F32)], axis=0)
    total = dot_nt(jnp.ones((8, LANES), F32), spread, HIGHEST)[0:1]
    high = total.astype(BF).astype(F32)
    middle = (total - high).astype(BF).astype(F32)
    low = total - high - middle
    cols = columns_ref[...]
    col_x = cols // GRID
    first = jnp.concatenate([col_x, cols - col_x * GRID], axis=1).astype(F32)
    other = jnp.concatenate([high, middle, low], axis=0)
    other = jnp.concatenate([other, jnp.zeros((3, LANES), F32)], axis=1)
    meta = jnp.concatenate([jnp.zeros((2 * DEPTH, 2 * LANES), F32), first, other], axis=0)
    lines = lines.reshape(PW, ROWS, 2 * LANES) + meta[None]
    lines_ref[...] = lines.astype(BF)
    load(lines_ref, send_hbm, sems.at[10]).wait()
    low_copy.wait()


def planes_kernel(
    recv_hbm,
    pot_hbm,
    spread_hbm,
    y_hbm,
    mix_in_hbm,
    mix_out_hbm,
    x_inv_hbm,
    x_fwd_hbm,
    fold_hbm,
    couple_ref,
    back_hbm,
    mixed_ref,
    recv_ref,
    pot_ref,
    spread_ref,
    y_ref,
    mix_in_ref,
    mix_out_ref,
    x_inv_ref,
    x_fwd_ref,
    fold_ref,
    back_ref,
    rows_ref,
    mask_ref,
    grid_ref,
    near_ref,
    far_ref,
    near_out_ref,
    far_out_ref,
    near_pot_ref,
    far_pot_ref,
    place_ref,
    index_ref,
    sems,
):
    pairs = (
        (recv_hbm, recv_ref),
        (spread_hbm, spread_ref),
        (y_hbm, y_ref),
        (mix_in_hbm, mix_in_ref),
        (x_inv_hbm, x_inv_ref),
        (x_fwd_hbm, x_fwd_ref),
        (mix_out_hbm, mix_out_ref),
        (fold_hbm, fold_ref),
        (pot_hbm, pot_ref),
    )
    copies = [load(a, b, sems.at[k]) for k, (a, b) in enumerate(pairs)]

    def clear(i, _):
        grid_ref[pl.ds(pl.multiple_of(i * 256, 256), 256), :] = jnp.zeros((256, LANES), F32)
        return 0

    lax.fori_loop(0, SPAN * GRID // 256, clear, 0)
    copies[0].wait()
    lane = lax.broadcasted_iota(jnp.int32, (1, LANES), 1)
    group_start = (lane // WIDTH * SPAN).astype(F32)
    source = lax.broadcasted_iota(jnp.int32, (PW, PW * ROWS), 0)
    entry = lax.broadcasted_iota(jnp.int32, (PW, PW * ROWS), 1)
    pick = (entry == source * ROWS + 2 * DEPTH).astype(F32).astype(BF)
    xy = dot(pick, recv_ref[...])
    x, y = xy[:, :LANES], xy[:, LANES:]
    for g in range(1, GROUPS):
        x = jnp.where(x >= SPAN, x - SPAN, x)
    place_ref[...] = (x * GRID + y).astype(jnp.int32)
    index_copy = load(place_ref, index_ref, sems.at[13])
    copies[1].wait()
    turned = recv_ref[...].astype(F32).T
    entry = lax.broadcasted_iota(jnp.int32, (32, PW * ROWS), 1)
    sums = jnp.where(entry % ROWS > 2 * DEPTH, turned[:32], 0.0)
    sums = jnp.sum(sums, axis=1, keepdims=True) + jnp.zeros((32, LANES), F32)
    mixed_ref[...] = dot(couple_ref[...], sums, HIGHEST)
    turned = turned.astype(BF)
    for s in range(8):
        for g in range(PW // 8):
            left = jnp.concatenate(
                [
                    turned[0:LANES, g * LANES : (g + 1) * LANES],
                    turned[LANES : 2 * LANES, g * LANES : (g + 1) * LANES],
                ],
                axis=1,
            )
            both = dot(left, spread_ref[s])
            start = (g * 8 + s) * LANES
            rows_ref[start : start + LANES, :] = both[:, :LANES]
            offset = both[:, LANES:] - group_start
            mask_ref[start : start + LANES, :] = jnp.where(
                (offset >= 0.0) & (offset < SPAN), 1.0, 0.0
            )

    index_copy.wait()

    def scatter(i, _):
        base = pl.multiple_of(i * LOCAL, LOCAL)
        for u in range(LOCAL):
            place = pl.ds(index_ref[i, u], 1)
            row = pl.ds(base + u, 1)
            pltpu.store(grid_ref.at[place, :], rows_ref[row, :], mask=mask_ref[row, :] > 0.5)
        return 0

    lax.fori_loop(0, PW, scatter, 0)
    for copy in copies[2:]:
        copy.wait()
    for zi in range(DEPTH):
        part = slice(zi * GRID, (zi + 1) * GRID)
        near_pot_ref[part, :] = pot_ref[zi, :, :LANES]
        far_pot_ref[part, :] = jnp.concatenate(
            [pot_ref[zi, :, LANES:], jnp.zeros((GRID, 2 * LANES - GRID), F32)], axis=1
        )

    def along_y_in(i, _):
        base = pl.multiple_of(i * 2 * GRID, 2 * GRID)
        pair = jnp.concatenate(
            [grid_ref[pl.ds(base, GRID), :], grid_ref[pl.ds(base + GRID, GRID), :]], axis=1
        ).astype(BF)
        both = dot(y_ref[...], pair).astype(BF)
        for h in range(2):
            part = jnp.concatenate(
                [
                    both[:GRID, h * LANES : (h + 1) * LANES],
                    both[GRID:, h * LANES : (h + 1) * LANES],
                ],
                axis=1,
            )
            mixed = dot_nt(mix_in_ref[...], part)
            place = pl.ds((2 * i + h) * STEP, LANES)
            near_ref[place, :] = mixed[:, :LANES]
            far_ref[place, :] = jnp.concatenate(
                [mixed[:, LANES:], jnp.zeros((LANES, 2 * LANES - GRID), F32)], axis=1
            )
        return 0

    lax.fori_loop(0, SPAN // 2, along_y_in, 0, unroll=True)

    for zi in range(DEPTH):
        for g in range(GROUPS):
            part = pl.ds(zi * GRID + g, SPAN, stride=GROUPS)
            pot = jnp.concatenate([near_pot_ref[part, :], far_pot_ref[part, :]], axis=1)
            pot = jnp.concatenate([pot, pot], axis=0)
            for b in range(BANDS):
                lane = g * WIDTH + b * 2 * DEPTH + zi
                places = [pl.ds(lane + ri * DEPTH, SPAN, stride=STEP) for ri in range(2)]
                plane = jnp.concatenate(
                    [
                        jnp.concatenate([ref[place, :] for place in places], axis=0)
                        for ref in (near_ref, far_ref)
                    ],
                    axis=1,
                ).astype(BF)
                field = (dot(x_inv_ref[g], plane) * pot).astype(BF)
                back = dot(x_fwd_ref[g], field)
                for ri, place in enumerate(places):
                    near_out_ref[place, :] = back[ri * SPAN : (ri + 1) * SPAN, :LANES]
                    far_out_ref[place, :] = back[ri * SPAN : (ri + 1) * SPAN, LANES:]

    def along_y_out(i, _):
        places = [pl.ds((2 * i + h) * STEP, LANES) for h in range(2)]
        pair = jnp.concatenate(
            [
                jnp.concatenate([near_out_ref[place, :] for place in places], axis=0),
                jnp.concatenate([far_out_ref[place, : GRID - LANES] for place in places], axis=0),
            ],
            axis=1,
        ).astype(BF)
        both = dot_nt(y_ref[...], pair).astype(BF)
        base = pl.multiple_of(i * 2 * GRID, 2 * GRID)
        for h in range(2):
            part = jnp.concatenate(
                [
                    both[:GRID, h * LANES : (h + 1) * LANES],
                    both[GRID:, h * LANES : (h + 1) * LANES],
                ],
                axis=1,
            )
            grid_ref[pl.ds(base + h * GRID, GRID), :] = dot(part, mix_out_ref[...])
        return 0

    lax.fori_loop(0, SPAN // 2, along_y_out, 0, unroll=True)

    def gather(i, _):
        base = pl.multiple_of(i * LOCAL, LOCAL)
        for u in range(LOCAL):
            rows_ref[pl.ds(base + u, 1), :] = grid_ref[pl.ds(index_ref[i, u], 1), :]
        return 0

    lax.fori_loop(0, PW, gather, 0)

    outs = []
    for d in range(PW):
        part = slice(d * LANES, (d + 1) * LANES)
        kept = (rows_ref[part, :] * mask_ref[part, :]).astype(BF)
        folded = dot_nt(fold_ref[...], kept).astype(BF)
        back_ref[d * ROWS : (d + 1) * ROWS, 0:LANES] = folded[:ROWS]
        back_ref[d * ROWS : (d + 1) * ROWS, LANES:] = folded[ROWS:]
        if d % 8 == 7:
            piece = pl.ds((d - 7) * ROWS, 8 * ROWS)
            outs.append(load(back_ref.at[piece], back_hbm.at[piece], sems.at[9 + d // 8]))
    for copy in outs:
        copy.wait()


def finish_kernel(
    back_hbm,
    table_hbm,
    block_hbm,
    beta_hbm,
    next_hbm,
    past_hbm,
    mixed_ref,
    columns_ref,
    applied_hbm,
    cross_ref,
    back_ref,
    table_ref,
    block_ref,
    beta_ref,
    next_ref,
    past_ref,
    local_ref,
    applied_ref,
    sems,
):
    pairs = (
        (back_hbm, back_ref),
        (table_hbm, table_ref),
        (block_hbm, block_ref),
        (beta_hbm, beta_ref),
        (next_hbm, next_ref),
        (past_hbm, past_ref),
    )
    copies = [load(a, b, sems.at[k]) for k, (a, b) in enumerate(pairs)]
    cols = columns_ref[...]
    col_x = cols // GRID
    fx = wrapped(col_x)
    fy = wrapped(cols - col_x * GRID)
    fxy = fx * fx + fy * fy
    copies[0].wait()
    copies[1].wait()
    local_ref[...] = dot(table_ref[0], back_ref[...]) + dot(table_ref[1], back_ref[...])
    for copy in copies[2:]:
        copy.wait()
    chunk = 48
    totals = [jnp.zeros((8, LANES), F32) for _ in range(16)]
    outs = []
    for start in range(0, GRID, chunk):
        part = slice(start, start + chunk)
        fz = wrapped(lax.broadcasted_iota(jnp.int32, (chunk, LANES), 0) + start)
        kinetic = (fz * fz + fxy).astype(F32) * (4.0 / (GRID * GRID))
        low = []
        for b in range(BANDS):
            real = local_ref[start : start + chunk, b * LANES : (b + 1) * LANES]
            imag = local_ref[GRID + start : GRID + start + chunk, b * LANES : (b + 1) * LANES]
            real = real + kinetic * block_ref[b, 0, part]
            imag = imag + kinetic * block_ref[b, 1, part]
            for k in range(PROJ):
                at = (b * PROJ + k) * 2
                mr, mi = mixed_ref[at : at + 1, :], mixed_ref[at + 1 : at + 2, :]
                br, bi = beta_ref[k, 0, part], beta_ref[k, 1, part]
                real = real + mr * br - mi * bi
                imag = imag + mr * bi + mi * br
            applied_ref[b, 0, part] = real
            applied_ref[b, 1, part] = imag
            low.append((real.astype(BF).astype(F32), imag.astype(BF).astype(F32)))
        outs.append(
            load(
                applied_ref.at[:, :, pl.ds(start, chunk)],
                applied_hbm.at[:, :, pl.ds(start, chunk)],
                sems.at[6 + start // chunk],
            )
        )
        for o, other in enumerate((next_ref, past_ref)):
            for m in range(BANDS):
                otr = other[m, 0, part].astype(F32)
                oti = other[m, 1, part].astype(F32)
                for n in range(BANDS):
                    ar, ai = low[n]
                    real = (otr * ar + oti * ai).reshape(chunk // 8, 8, LANES).sum(0)
                    imag = (otr * ai - oti * ar).reshape(chunk // 8, 8, LANES).sum(0)
                    totals[o * 8 + m * 2 + n] += real
                    totals[o * 8 + 4 + m * 2 + n] += imag
    stacked = jnp.concatenate([jnp.sum(t, axis=0, keepdims=True) for t in totals], axis=0)
    spread = jnp.concatenate([stacked, jnp.zeros((LANES - 16, LANES), F32)], axis=0)
    cross_ref[...] = dot_nt(jnp.ones((8 * PW, LANES), F32), spread, HIGHEST)
    for copy in outs:
        copy.wait()


def from_behind(value, axis, steps):
    count = lax.axis_size(axis)
    first, last = max(0, -steps), min(count, count - steps)
    return lax.ppermute(value, axis, [(s, s + steps) for s in range(first, last)])


def vmem():
    return pl.BlockSpec(memory_space=pltpu.VMEM)


def hbm():
    return pl.BlockSpec(memory_space=pltpu.HBM)


def smem():
    return pl.BlockSpec(memory_space=pltpu.SMEM)


def exchange(value):
    return lax.all_to_all(value, "pw", split_axis=0, concat_axis=0, tiled=True)


def planes_call(recv, potential, half, couple, name="planes"):
    return pl.pallas_call(
        planes_kernel,
        name=name,
        out_shape=(
            jax.ShapeDtypeStruct((PW * ROWS, 2 * LANES), BF),
            jax.ShapeDtypeStruct((32, LANES), F32),
        ),
        in_specs=[hbm()] * 9 + [vmem()],
        out_specs=(hbm(), vmem()),
        scratch_shapes=[
            pltpu.VMEM((PW * ROWS, 2 * LANES), BF),
            pltpu.VMEM((DEPTH, GRID, GRID), F32),
        ]
        + [
            pltpu.VMEM(half[k].shape, BF)
            for k in ("spread", "y_table", "mix_in", "mix_out", "x_inverse", "x_forward", "fold")
        ]
        + [
            pltpu.VMEM((PW * ROWS, 2 * LANES), BF),
            pltpu.VMEM((COLS, LANES), F32),
            pltpu.VMEM((COLS, LANES), F32),
            pltpu.VMEM((SPAN * GRID, LANES), F32),
            pltpu.VMEM((SPAN * STEP, LANES), F32),
            pltpu.VMEM((SPAN * STEP, LANES), F32),
            pltpu.VMEM((SPAN * STEP, LANES), F32),
            pltpu.VMEM((SPAN * STEP, LANES), F32),
            pltpu.VMEM((DEPTH * GRID, LANES), F32),
            pltpu.VMEM((DEPTH * GRID, LANES), F32),
            pltpu.VMEM((PW, LOCAL), jnp.int32),
            pltpu.SMEM((PW, LOCAL), jnp.int32),
            pltpu.SemaphoreType.DMA((14,)),
        ],
        compiler_params=pltpu.CompilerParams(vmem_limit_bytes=64 << 20),
        cost_estimate=pl.CostEstimate(
            flops=20_000_000_000, bytes_accessed=4 << 20, transcendentals=0
        ),
    )(
        recv,
        potential,
        half["spread"],
        half["y_table"],
        half["mix_in"],
        half["mix_out"],
        half["x_inverse"],
        half["x_forward"],
        half["fold"],
        couple,
    )


def two_parts(exact):
    high = np.asarray(exact).astype(jnp.bfloat16).astype(np.float64)
    return jnp.asarray(np.stack([high, exact - high]), BF)


def per_device(orbitals, potential, projectors, coupling, columns):
    tables = build_tables()
    half = {k: jnp.asarray(v, BF) for k, v in tables.items()}
    block = orbitals[0]
    own_columns = columns.reshape(1, LOCAL)
    scale = 1.0 / math.sqrt(COLS * GRID)
    coupling_sym = 0.5 * (coupling + coupling.T)
    couple = jnp.einsum(
        "bc,jk,rs->bkrcjs",
        jnp.eye(BANDS, dtype=F32),
        coupling_sym * scale,
        jnp.eye(2, dtype=F32),
        precision=HIGHEST,
    ).reshape(32, 32)

    sent, low_orbitals = pl.pallas_call(
        send_kernel,
        name="lines_out",
        out_shape=(
            jax.ShapeDtypeStruct((PW, ROWS, 2 * LANES), BF),
            jax.ShapeDtypeStruct((BANDS, 2, GRID, LOCAL), BF),
        ),
        in_specs=[hbm(), hbm(), vmem(), hbm()],
        out_specs=(hbm(), hbm()),
        scratch_shapes=[
            pltpu.VMEM((BANDS, 2, GRID, LOCAL), F32),
            pltpu.VMEM((PROJ, 2, GRID, LOCAL), F32),
            pltpu.VMEM((2, PW * ROWS, 2 * GRID), BF),
            pltpu.VMEM((PW, ROWS, 2 * LANES), BF),
            pltpu.VMEM((BANDS, 2, GRID, LOCAL), BF),
            pltpu.SemaphoreType.DMA((12,)),
        ],
        compiler_params=pltpu.CompilerParams(vmem_limit_bytes=64 << 20),
    )(block, projectors, own_columns, two_parts(tables["to_planes"]))
    recv = exchange(sent)
    recv, low_orbitals = lax.optimization_barrier((recv, low_orbitals))
    following = from_behind(low_orbitals, "band", -1)
    preceding = from_behind(low_orbitals, "band", 2)

    back, mixed = planes_call(recv.reshape(PW * ROWS, 2 * LANES), potential, half, couple)
    returned = exchange(back.reshape(PW, ROWS, 2 * LANES)).reshape(PW * ROWS, 2 * LANES)

    applied, cross = pl.pallas_call(
        finish_kernel,
        name="lines_in",
        out_shape=(
            jax.ShapeDtypeStruct((BANDS, 2, GRID, LOCAL), F32),
            jax.ShapeDtypeStruct((8 * PW, LANES), F32),
        ),
        in_specs=[hbm()] * 6 + [vmem()] * 2,
        out_specs=(hbm(), vmem()),
        scratch_shapes=[
            pltpu.VMEM((PW * ROWS, 2 * LANES), BF),
            pltpu.VMEM((2, 2 * GRID, PW * ROWS), BF),
            pltpu.VMEM((BANDS, 2, GRID, LOCAL), F32),
            pltpu.VMEM((PROJ, 2, GRID, LOCAL), F32),
            pltpu.VMEM((BANDS, 2, GRID, LOCAL), BF),
            pltpu.VMEM((BANDS, 2, GRID, LOCAL), BF),
            pltpu.VMEM((2 * GRID, 2 * LANES), F32),
            pltpu.VMEM((BANDS, 2, GRID, LOCAL), F32),
            pltpu.SemaphoreType.DMA((10,)),
        ],
        compiler_params=pltpu.CompilerParams(vmem_limit_bytes=64 << 20),
    )(
        returned,
        two_parts(tables["from_planes"]),
        block,
        projectors,
        following,
        preceding,
        mixed,
        own_columns,
    )
    every = lax.all_to_all(cross, ("band", "pw"), split_axis=0, concat_axis=0, tiled=True)
    blocks = lax.axis_size("band")
    sums = jnp.sum(every[:, :16].reshape(blocks, PW, 16), axis=1) * scale
    rows = lax.axis_index("band") + jnp.asarray([0, -1, 0, 2], jnp.int32)
    picked = jnp.where(
        (rows[:, None] == jnp.arange(blocks)[None, :])[:, :, None], sums[None], 0.0
    ).sum(1)
    picked = picked.reshape(4, 2, 2, BANDS, BANDS)
    sign = jnp.asarray([1.0, -1.0], F32).reshape(2, 1, 1)
    adjoint = lambda v: jnp.swapaxes(v, 1, 2) * sign
    cross_terms = jnp.stack(
        [picked[2, 1], adjoint(picked[1, 0]), picked[0, 0], adjoint(picked[3, 1])]
    )
    return applied[None], cross_terms[None]


def solution(mesh):
    return jax.shard_map(
        per_device,
        mesh=mesh,
        in_specs=(
            P("band", None, None, None, "pw"),
            P("pw", None, None),
            P(None, None, None, "pw"),
            P(),
            P("pw"),
        ),
        out_specs=(P("band", None, None, None, "pw"), P("band", None, None, None, None)),
        check_vma=False,
    )
```

time: 125 us -> 105 us (0.84)
  the two profiles are of different devices: /device:TPU:3 before, /device:TPU:1 now
where the time goes in v2:
time: 105 us; the launch traced here: 104 us
  starting transfers between devices  45.3 us (43%)
  Pallas kernels  28.6 us (27%)
  waiting for transfers between devices  24.4 us (23%)
  local copies, waits for them, and re-layouts  2.73 us (3%)
  other arithmetic  2.44 us (2%)
    all_to_all x1, starting transfers between devices, per_device(): lax.all_to_all(cross, ('band', 'pw'), split_axis=0, concat_axis=0, tiled=...  23.1 us
    pallas_call x1, Pallas kernels, planes_call(): pl.pallas_call(planes_kernel, name=name, out_shape=(jax.ShapeDtypeStruct(...  19.5 us
    all_to_all x2, starting transfers between devices, exchange(): return lax.all_to_all(value, 'pw', split_axis=0, concat_axis=0, tiled=True)  14.7 us
    all_to_all x1, waiting for transfers between devices, per_device(): lax.all_to_all(cross, ('band', 'pw'), split_axis=0, concat_axis=0, tiled=...  11.9 us
    all_to_all x2, waiting for transfers between devices, exchange(): return lax.all_to_all(value, 'pw', split_axis=0, concat_axis=0, tiled=True)  9.32 us
    ppermute x2, starting transfers between devices, from_behind(): lax.ppermute(value, axis, [(s, s + steps) for s in range(first, last)])  7.49 us
    pallas_call x1, Pallas kernels, per_device(): pl.pallas_call(finish_kernel, name='lines_in', out_shape=(jax.ShapeDtypeS...  4.92 us
    pallas_call x1, Pallas kernels, per_device(): pl.pallas_call(send_kernel, name='lines_out', out_shape=(jax.ShapeDtypeSt...  4.14 us
  transfers between devices with their start and end apart: 5, of which 5 were waited for; matrix products, arithmetic and copies ran while one was open for 3% of the time, Pallas kernels for 0%

profile of v2, /device:TPU:1, one launch (start us, length us, event | category | flops | bytes accessed | tf_op | source)
XLA Modules:
  0.0 104.2 jit_solution(9804309300228450591)
XLA Ops:
  0.6 4.1 %lines_out.1 = (bf16[32,16,256]{2,1,0:T(8,128)(2,1)}, bf16[2,2,192,128]{3,2,1,0:T(8,128)(2,1)}) custom-call(f32[2,2,192,128]{3,2,1,0:T(8,128)} %bitcast.30, f32[8,2,192,128]{3,2,1,0:T(8,128)} %beta_hbm.3, s32[1,128]{1,0:T(1,128)} %bitcast.41, bf16[2,512,384]{2,1,0:T(8,128)(2,1)} %constant.43.clone.table_hbm), custom_call_target="tpu_custom_call" | custom-call | tf_op jit(solution)/shard_map/lines_out/pallas_call | solution.py:555
  4.8 10.3 %all-to-all-start = ((bf16[32,16,256]{2,1,0:T(8,128)(2,1)}), bf16[32,16,256]{2,1,0:T(8,128)(2,1)}, u32[]{:S(2)}, u32[]{:S(2)}) async-start(bf16[32,16,256]{2,1,0:T(8,128)(2,1)} %get-tuple-element.10), calls=%async_computation | async-start | bytes 524288 | tf_op jit(solution)/shard_map/all_to_all | solution.py:481
  15.0 0.8 copy.34
  15.8 0.7 fusion
  16.5 0.1 copy.35
  16.6 0.1 broadcast_multiply_fusion.1
  16.6 0.1 multiply_bitcast_fusion
  16.7 0.7 reshape.55.couple_ref
  17.5 8.7 %all-to-all-done = bf16[32,16,256]{2,1,0:T(8,128)(2,1)} async-done(((bf16[32,16,256]{2,1,0:T(8,128)(2,1)}), bf16[32,16,256]{2,1,0:T(8,128)(2,1)}, u32[]{:S(2)}, u32[]{:S(2)}) %all-to-all-start) | async-done | bytes 262176 | tf_op jit(solution)/shard_map/all_to_all | solution.py:481
  26.2 19.5 %planes.1 = (bf16[512,256]{1,0:T(8,128)(2,1)}, f32[32,128]{1,0:T(8,128)}) custom-call(bf16[512,256]{1,0:T(8,128)(2,1)} %bitcast.2.recv_hbm, f32[6,192,192]{2,1,0:T(8,128)} %pot_hbm.1, bf16[8,256,256]{2,1,0:T(8,128)(2,1)} %constant.36.clone.spread_hbm, bf16[384,192]{1,0:T(8,128)(2,1)} %constant.37.clone.y_hbm, bf16[128,256]{1,0:T(8,128)(2,1)} %constant.38.clone.mix_in_hbm, ...), custom_call_target="tpu_custom_call" | custom-call | flops 20000000000 | bytes 4194304 | tf_op jit(solution)/shard_map/planes/pallas_call | solution.py:485
  45.8 4.4 %all-to-all-start.1 = ((bf16[32,16,256]{2,1,0:T(8,128)(2,1)}), bf16[32,16,256]{2,1,0:T(8,128)(2,1)}, u32[]{:S(2)}, u32[]{:S(2)}) async-start(bf16[32,16,256]{2,1,0:T(8,128)(2,1)} %bitcast.33), calls=%async_computation.1 | async-start | bytes 524288 | tf_op jit(solution)/shard_map/all_to_all | solution.py:481
  50.2 1.3 %collective-permute-start = (bf16[2,2,192,128]{3,2,1,0:T(8,128)(2,1)}, bf16[2,2,192,128]{3,2,1,0:T(8,128)(2,1)}, u32[]{:S(2)}, u32[]{:S(2)}) collective-permute-start(bf16[2,2,192,128]{3,2,1,0:T(8,128)(2,1)} %get-tuple-element.14), channel_id=1, source_target_pairs={{32,0},{64,32},{96,64},{128,96},{160,128},{192,160},{224,192},{33,... | collective-permute-start | bytes 589832 | tf_op jit(solution)/shard_map/ppermute | solution.py:465
  51.5 6.2 %collective-permute-start.1 = (bf16[2,2,192,128]{3,2,1,0:T(8,128)(2,1)}, bf16[2,2,192,128]{3,2,1,0:T(8,128)(2,1)}, u32[]{:S(2)}, u32[]{:S(2)}) collective-permute-start(bf16[2,2,192,128]{3,2,1,0:T(8,128)(2,1)} %get-tuple-element.14), channel_id=1, source_target_pairs={{0,64},{32,96},{64,128},{96,160},{128,192},{160,224},{1,65},{33,97... | collective-permute-start | bytes 589832 | tf_op jit(solution)/shard_map/ppermute | solution.py:465
  57.7 0.8 collective-permute-done.next_hbm
  58.5 2.4 %collective-permute-done.1.past_hbm = bf16[2,2,192,128]{3,2,1,0:T(8,128)(2,1)} collective-permute-done((bf16[2,2,192,128]{3,2,1,0:T(8,128)(2,1)}, bf16[2,2,192,128]{3,2,1,0:T(8,128)(2,1)}, u32[]{:S(2)}, u32[]{:S(2)}) %collective-permute-start.1) | collective-permute-done | bytes 196640 | tf_op jit(solution)/shard_map/ppermute | solution.py:465
  60.8 0.6 all-to-all-done.1
  61.4 4.9 %lines_in.1 = (f32[2,2,192,128]{3,2,1,0:T(8,128)}, f32[256,128]{1,0:T(8,128)}) custom-call(bf16[512,256]{1,0:T(8,128)(2,1)} %bitcast.6.back_hbm, bf16[2,384,512]{2,1,0:T(8,128)(2,1)} %constant.44.clone.table_hbm, f32[2,2,192,128]{3,2,1,0:T(8,128)} %bitcast.31, f32[8,2,192,128]{3,2,1,0:T(8,128)} %beta_hbm.3, ...), custom_call_target="tpu_custom_call" | custom-call | tf_op jit(solution)/shard_map/lines_in/pallas_call | solution.py:582
  66.4 23.1 %all-to-all-start.2 = ((f32[256,1,128]{2,1,0:T(1,128)}), f32[256,1,128]{2,1,0:T(1,128)S(1)}, u32[]{:S(2)}, u32[]{:S(2)}) async-start(f32[256,1,128]{2,1,0:T(1,128)} %bitcast.34), calls=%async_computation.2 | async-start | bytes 262144 | tf_op jit(solution)/shard_map/all_to_all | solution.py:613
  89.5 0.7 broadcast_add_fusion
  90.2 0.1 iota_compare_fusion
  90.2 11.9 %all-to-all-done.2 = f32[256,1,128]{2,1,0:T(1,128)S(1)} async-done(((f32[256,1,128]{2,1,0:T(1,128)}), f32[256,1,128]{2,1,0:T(1,128)S(1)}, u32[]{:S(2)}, u32[]{:S(2)}) %all-to-all-start.2) | async-done | bytes 131104 | tf_op jit(solution)/shard_map/all_to_all | solution.py:613
  102.2 0.1 select_reduce_fusion
  102.3 0.1 copy.37
  102.4 0.2 slice_reduce_fusion.3
  102.6 0.7 multiply_bitcast_fusion.2
  103.3 0.1 copy.38
  103.4 0.1 copy.39
  103.5 0.7 copy.40
  (4 shorter events, 0.0 us)
Async XLA Ops:
  4.8 21.4 %all-to-all-start = ((bf16[32,16,256]{2,1,0:T(8,128)(2,1)}), bf16[32,16,256]{2,1,0:T(8,128)(2,1)}, u32[]{:S(2)}, u32[]{:S(2)}) async-start(bf16[32,16,256]{2,1,0:T(8,128)(2,1)} %get-tuple-element.10), calls=%async_computation | async-start | bytes 524288 | tf_op jit(solution)/shard_map/all_to_all | solution.py:481
  45.8 15.7 %all-to-all-start.1 = ((bf16[32,16,256]{2,1,0:T(8,128)(2,1)}), bf16[32,16,256]{2,1,0:T(8,128)(2,1)}, u32[]{:S(2)}, u32[]{:S(2)}) async-start(bf16[32,16,256]{2,1,0:T(8,128)(2,1)} %bitcast.33), calls=%async_computation.1 | async-start | bytes 524288 | tf_op jit(solution)/shard_map/all_to_all | solution.py:481
  50.2 8.3 %collective-permute-start = (bf16[2,2,192,128]{3,2,1,0:T(8,128)(2,1)}, bf16[2,2,192,128]{3,2,1,0:T(8,128)(2,1)}, u32[]{:S(2)}, u32[]{:S(2)}) collective-permute-start(bf16[2,2,192,128]{3,2,1,0:T(8,128)(2,1)} %get-tuple-element.14), channel_id=1, source_target_pairs={{32,0},{64,32},{96,64},{128,96},{160,128},{192,160},{224,192},{33,... | collective-permute-start | bytes 589832 | tf_op jit(solution)/shard_map/ppermute | solution.py:465
  51.5 9.4 %collective-permute-start.1 = (bf16[2,2,192,128]{3,2,1,0:T(8,128)(2,1)}, bf16[2,2,192,128]{3,2,1,0:T(8,128)(2,1)}, u32[]{:S(2)}, u32[]{:S(2)}) collective-permute-start(bf16[2,2,192,128]{3,2,1,0:T(8,128)(2,1)} %get-tuple-element.14), channel_id=1, source_target_pairs={{0,64},{32,96},{64,128},{96,160},{128,192},{160,224},{1,65},{33,97... | collective-permute-start | bytes 589832 | tf_op jit(solution)/shard_map/ppermute | solution.py:465
  66.4 35.8 %all-to-all-start.2 = ((f32[256,1,128]{2,1,0:T(1,128)}), f32[256,1,128]{2,1,0:T(1,128)S(1)}, u32[]{:S(2)}, u32[]{:S(2)}) async-start(f32[256,1,128]{2,1,0:T(1,128)} %bitcast.34), calls=%async_computation.2 | async-start | bytes 262144 | tf_op jit(solution)/shard_map/all_to_all | solution.py:613

commit v3 on v2

--- a/solution.py
+++ b/solution.py
@@ -182,7 +182,7 @@
     x_inv_hbm,
     x_fwd_hbm,
     fold_hbm,
-    couple_ref,
+    coupling_ref,
     back_hbm,
     mixed_ref,
     recv_ref,
@@ -243,7 +243,16 @@
     entry = lax.broadcasted_iota(jnp.int32, (32, PW * ROWS), 1)
     sums = jnp.where(entry % ROWS > 2 * DEPTH, turned[:32], 0.0)
     sums = jnp.sum(sums, axis=1, keepdims=True) + jnp.zeros((32, LANES), F32)
-    mixed_ref[...] = dot(couple_ref[...], sums, HIGHEST)
+    row = lax.broadcasted_iota(jnp.int32, (32, 32), 0)
+    column = lax.broadcasted_iota(jnp.int32, (32, 32), 1)
+    same = (row // (2 * PROJ) == column // (2 * PROJ)) & (row % 2 == column % 2)
+    row = lax.broadcasted_iota(jnp.int32, (32, PROJ), 0)
+    column = lax.broadcasted_iota(jnp.int32, (32, PROJ), 1)
+    widen = (row // 2 % PROJ == column).astype(F32)
+    coupling = coupling_ref[...]
+    couple = dot_nt(dot(widen, 0.5 * (coupling + coupling.T), HIGHEST), widen, HIGHEST)
+    couple = jnp.where(same, couple * (1.0 / math.sqrt(COLS * GRID)), 0.0)
+    mixed_ref[...] = dot(couple, sums, HIGHEST)
     turned = turned.astype(BF)
     for s in range(8):
         for g in range(PW // 8):
@@ -378,18 +387,19 @@
     table_hbm,
     block_hbm,
     beta_hbm,
-    next_hbm,
-    past_hbm,
     mixed_ref,
     columns_ref,
+    other_0,
+    other_1,
+    other_2,
+    other_3,
     applied_hbm,
     cross_ref,
     back_ref,
     table_ref,
     block_ref,
     beta_ref,
-    next_ref,
-    past_ref,
+    others_ref,
     local_ref,
     applied_ref,
     sems,
@@ -399,8 +409,10 @@
         (table_hbm, table_ref),
         (block_hbm, block_ref),
         (beta_hbm, beta_ref),
-        (next_hbm, next_ref),
-        (past_hbm, past_ref),
+        (other_0, others_ref.at[0]),
+        (other_1, others_ref.at[1]),
+        (other_2, others_ref.at[2]),
+        (other_3, others_ref.at[3]),
     )
     copies = [load(a, b, sems.at[k]) for k, (a, b) in enumerate(pairs)]
     cols = columns_ref[...]
@@ -414,7 +426,7 @@
     for copy in copies[2:]:
         copy.wait()
     chunk = 48
-    totals = [jnp.zeros((8, LANES), F32) for _ in range(16)]
+    totals = [jnp.zeros((8, LANES), F32) for _ in range(32)]
     outs = []
     for start in range(0, GRID, chunk):
         part = slice(start, start + chunk)
@@ -439,13 +451,13 @@
             load(
                 applied_ref.at[:, :, pl.ds(start, chunk)],
                 applied_hbm.at[:, :, pl.ds(start, chunk)],
-                sems.at[6 + start // chunk],
+                sems.at[8 + start // chunk],
             )
         )
-        for o, other in enumerate((next_ref, past_ref)):
+        for o in range(4):
             for m in range(BANDS):
-                otr = other[m, 0, part].astype(F32)
-                oti = other[m, 1, part].astype(F32)
+                otr = others_ref[o, m, 0, part].astype(F32)
+                oti = others_ref[o, m, 1, part].astype(F32)
                 for n in range(BANDS):
                     ar, ai = low[n]
                     real = (otr * ar + oti * ai).reshape(chunk // 8, 8, LANES).sum(0)
@@ -453,16 +465,15 @@
                     totals[o * 8 + m * 2 + n] += real
                     totals[o * 8 + 4 + m * 2 + n] += imag
     stacked = jnp.concatenate([jnp.sum(t, axis=0, keepdims=True) for t in totals], axis=0)
-    spread = jnp.concatenate([stacked, jnp.zeros((LANES - 16, LANES), F32)], axis=0)
-    cross_ref[...] = dot_nt(jnp.ones((8 * PW, LANES), F32), spread, HIGHEST)
+    spread = jnp.concatenate([stacked, jnp.zeros((LANES - 32, LANES), F32)], axis=0)
+    cross_ref[...] = dot_nt(jnp.ones((PW, LANES), F32), spread, HIGHEST)
     for copy in outs:
         copy.wait()
 
 
-def from_behind(value, axis, steps):
+def around(value, axis, steps):
     count = lax.axis_size(axis)
-    first, last = max(0, -steps), min(count, count - steps)
-    return lax.ppermute(value, axis, [(s, s + steps) for s in range(first, last)])
+    return lax.ppermute(value, axis, [(s, (s + steps) % count) for s in range(count)])
 
 
 def vmem():
@@ -481,7 +492,7 @@
     return lax.all_to_all(value, "pw", split_axis=0, concat_axis=0, tiled=True)
 
 
-def planes_call(recv, potential, half, couple, name="planes"):
+def planes_call(recv, potential, half, coupling, name="planes"):
     return pl.pallas_call(
         planes_kernel,
         name=name,
@@ -528,7 +539,7 @@
         half["x_inverse"],
         half["x_forward"],
         half["fold"],
-        couple,
+        coupling,
     )
 
 
@@ -543,15 +554,6 @@
     block = orbitals[0]
     own_columns = columns.reshape(1, LOCAL)
     scale = 1.0 / math.sqrt(COLS * GRID)
-    coupling_sym = 0.5 * (coupling + coupling.T)
-    couple = jnp.einsum(
-        "bc,jk,rs->bkrcjs",
-        jnp.eye(BANDS, dtype=F32),
-        coupling_sym * scale,
-        jnp.eye(2, dtype=F32),
-        precision=HIGHEST,
-    ).reshape(32, 32)
-
     sent, low_orbitals = pl.pallas_call(
         send_kernel,
         name="lines_out",
@@ -573,10 +575,11 @@
     )(block, projectors, own_columns, two_parts(tables["to_planes"]))
     recv = exchange(sent)
     recv, low_orbitals = lax.optimization_barrier((recv, low_orbitals))
-    following = from_behind(low_orbitals, "band", -1)
-    preceding = from_behind(low_orbitals, "band", 2)
-
-    back, mixed = planes_call(recv.reshape(PW * ROWS, 2 * LANES), potential, half, couple)
+    offsets = (-2, -1, 1, 2)
+    others = [around(low_orbitals, "band", -offset) for offset in offsets]
+
+    back, mixed = planes_call(recv.reshape(PW * ROWS, 2 * LANES), potential, half, coupling)
+    back, others = lax.optimization_barrier((back, others))
     returned = exchange(back.reshape(PW, ROWS, 2 * LANES)).reshape(PW * ROWS, 2 * LANES)
 
     applied, cross = pl.pallas_call(
@@ -584,20 +587,19 @@
         name="lines_in",
         out_shape=(
             jax.ShapeDtypeStruct((BANDS, 2, GRID, LOCAL), F32),
-            jax.ShapeDtypeStruct((8 * PW, LANES), F32),
+            jax.ShapeDtypeStruct((PW, LANES), F32),
         ),
-        in_specs=[hbm()] * 6 + [vmem()] * 2,
+        in_specs=[hbm()] * 4 + [vmem()] * 2 + [hbm()] * 4,
         out_specs=(hbm(), vmem()),
         scratch_shapes=[
             pltpu.VMEM((PW * ROWS, 2 * LANES), BF),
             pltpu.VMEM((2, 2 * GRID, PW * ROWS), BF),
             pltpu.VMEM((BANDS, 2, GRID, LOCAL), F32),
             pltpu.VMEM((PROJ, 2, GRID, LOCAL), F32),
-            pltpu.VMEM((BANDS, 2, GRID, LOCAL), BF),
-            pltpu.VMEM((BANDS, 2, GRID, LOCAL), BF),
+            pltpu.VMEM((4, BANDS, 2, GRID, LOCAL), BF),
             pltpu.VMEM((2 * GRID, 2 * LANES), F32),
             pltpu.VMEM((BANDS, 2, GRID, LOCAL), F32),
-            pltpu.SemaphoreType.DMA((10,)),
+            pltpu.SemaphoreType.DMA((12,)),
         ],
         compiler_params=pltpu.CompilerParams(vmem_limit_bytes=64 << 20),
     )(
@@ -605,24 +607,15 @@
         two_parts(tables["from_planes"]),
         block,
         projectors,
-        following,
-        preceding,
         mixed,
         own_columns,
-    )
-    every = lax.all_to_all(cross, ("band", "pw"), split_axis=0, concat_axis=0, tiled=True)
-    blocks = lax.axis_size("band")
-    sums = jnp.sum(every[:, :16].reshape(blocks, PW, 16), axis=1) * scale
-    rows = lax.axis_index("band") + jnp.asarray([0, -1, 0, 2], jnp.int32)
-    picked = jnp.where(
-        (rows[:, None] == jnp.arange(blocks)[None, :])[:, :, None], sums[None], 0.0
-    ).sum(1)
-    picked = picked.reshape(4, 2, 2, BANDS, BANDS)
-    sign = jnp.asarray([1.0, -1.0], F32).reshape(2, 1, 1)
-    adjoint = lambda v: jnp.swapaxes(v, 1, 2) * sign
-    cross_terms = jnp.stack(
-        [picked[2, 1], adjoint(picked[1, 0]), picked[0, 0], adjoint(picked[3, 1])]
-    )
+        *others,
+    )
+    every = exchange(cross)
+    summed = jnp.sum(every[:, :32], axis=0).reshape(4, 2, BANDS, BANDS)
+    source = lax.axis_index("band") + np.asarray(offsets, np.int32)
+    inside = (source >= 0) & (source < lax.axis_size("band"))
+    cross_terms = jnp.where(inside[:, None, None, None], summed * scale, 0.0)
     return applied[None], cross_terms[None]
 
 

time: 105 us -> 91.1 us (0.87)
  the two profiles are of different devices: /device:TPU:1 before, /device:TPU:5 now
where the time goes in v3:
time: 91.1 us; the launch traced here: 90.6 us
  Pallas kernels  28.9 us (32%)
  blocking collectives  20.6 us (23%)
  waiting for transfers between devices  19.7 us (22%)
  starting transfers between devices  19.1 us (21%)
    all_to_all x1, blocking collectives, exchange(): return lax.all_to_all(value, 'pw', split_axis=0, concat_axis=0, tiled=True)  20.6 us
    pallas_call x1, Pallas kernels, planes_call(): pl.pallas_call(planes_kernel, name=name, out_shape=(jax.ShapeDtypeStruct(...  19.7 us
    all_to_all x2, waiting for transfers between devices, exchange(): return lax.all_to_all(value, 'pw', split_axis=0, concat_axis=0, tiled=True)  18 us
    ppermute x4, starting transfers between devices, around(): lax.ppermute(value, axis, [(s, (s + steps) % count) for s in range(count)])  10.5 us
    all_to_all x2, starting transfers between devices, exchange(): return lax.all_to_all(value, 'pw', split_axis=0, concat_axis=0, tiled=True)  8.65 us
    pallas_call x1, Pallas kernels, per_device(): pl.pallas_call(finish_kernel, name='lines_in', out_shape=(jax.ShapeDtypeS...  5.1 us
    pallas_call x1, Pallas kernels, per_device(): pl.pallas_call(send_kernel, name='lines_out', out_shape=(jax.ShapeDtypeSt...  4.14 us
  transfers between devices with their start and end apart: 6, of which 3 were waited for; matrix products, arithmetic and copies ran while one was open for 1% of the time, Pallas kernels for 22%

profile of v3, /device:TPU:5, one launch (start us, length us, event | category | flops | bytes accessed | tf_op | source)
XLA Modules:
  0.0 90.6 jit_solution(13559351430848430025)
XLA Ops:
  0.6 4.1 %lines_out.1 = (bf16[32,16,256]{2,1,0:T(8,128)(2,1)}, bf16[2,2,192,128]{3,2,1,0:T(8,128)(2,1)}) custom-call(f32[2,2,192,128]{3,2,1,0:T(8,128)} %bitcast.10, f32[8,2,192,128]{3,2,1,0:T(8,128)} %beta_hbm.3, s32[1,128]{1,0:T(1,128)} %bitcast.16, bf16[2,512,384]{2,1,0:T(8,128)(2,1)} %constant.41.clone.table_hbm), custom_call_target="tpu_custom_call" | custom-call | tf_op jit(solution)/shard_map/lines_out/pallas_call | solution.py:557
  4.8 20.6 %all_to_all.22 = bf16[32,16,256]{2,1,0:T(8,128)(2,1)} all-to-all(bf16[32,16,256]{2,1,0:T(8,128)(2,1)} %get-tuple-element.15), channel_id=1, replica_groups=mesh['band'=8,'pw'=32] {'pw'}, dimensions={0} | all-to-all | bytes 524288 | tf_op jit(solution)/shard_map/all_to_all | solution.py:492
  25.4 4.2 %collective-permute-start = (bf16[2,2,192,128]{3,2,1,0:T(8,128)(2,1)}, bf16[2,2,192,128]{3,2,1,0:T(8,128)(2,1)}, u32[]{:S(2)}, u32[]{:S(2)}) collective-permute-start(bf16[2,2,192,128]{3,2,1,0:T(8,128)(2,1)} %get-tuple-element.19), channel_id=1, source_target_pairs={{0,64},{32,96},{64,128},{96,160},{128,192},{160,224},{192,0},{224,... | collective-permute-start | bytes 589832 | tf_op jit(solution)/shard_map/ppermute | solution.py:476
  29.5 1.8 %collective-permute-start.1 = (bf16[2,2,192,128]{3,2,1,0:T(8,128)(2,1)}, bf16[2,2,192,128]{3,2,1,0:T(8,128)(2,1)}, u32[]{:S(2)}, u32[]{:S(2)}) collective-permute-start(bf16[2,2,192,128]{3,2,1,0:T(8,128)(2,1)} %get-tuple-element.19), channel_id=1, source_target_pairs={{0,32},{32,64},{64,96},{96,128},{128,160},{160,192},{192,224},{224... | collective-permute-start | bytes 589832 | tf_op jit(solution)/shard_map/ppermute | solution.py:476
  31.3 0.0 collective-permute-start.2
  31.3 4.5 %collective-permute-start.3 = (bf16[2,2,192,128]{3,2,1,0:T(8,128)(2,1)}, bf16[2,2,192,128]{3,2,1,0:T(8,128)(2,1)}, u32[]{:S(2)}, u32[]{:S(2)}) collective-permute-start(bf16[2,2,192,128]{3,2,1,0:T(8,128)(2,1)} %get-tuple-element.19), channel_id=1, source_target_pairs={{0,192},{32,224},{64,0},{96,32},{128,64},{160,96},{192,128},{224,1... | collective-permute-start | bytes 589832 | tf_op jit(solution)/shard_map/ppermute | solution.py:476
  35.8 19.7 %planes.1 = (bf16[512,256]{1,0:T(8,128)(2,1)}, f32[32,128]{1,0:T(8,128)}) custom-call(bf16[512,256]{1,0:T(8,128)(2,1)} %bitcast.13, f32[6,192,192]{2,1,0:T(8,128)} %pot_hbm.1, bf16[8,256,256]{2,1,0:T(8,128)(2,1)} %constant.34.clone.spread_hbm, bf16[384,192]{1,0:T(8,128)(2,1)} %constant.35.clone.y_hbm, bf16[128,256]{1,0:T(8,128)(2,1)} %constant.36.clone.mix_in_hbm, ...), custom_call_target="tpu_custom_call" | custom-call | flops 20000000000 | bytes 4194304 | tf_op jit(solution)/shard_map/planes/pallas_call | solution.py:496
  55.5 0.0 collective-permute-done.other_0
  55.5 0.0 collective-permute-done.1.other_1
  55.5 0.0 collective-permute-done.2.other_2
  55.6 1.7 %collective-permute-done.3.other_3 = bf16[2,2,192,128]{3,2,1,0:T(8,128)(2,1)} collective-permute-done((bf16[2,2,192,128]{3,2,1,0:T(8,128)(2,1)}, bf16[2,2,192,128]{3,2,1,0:T(8,128)(2,1)}, u32[]{:S(2)}, u32[]{:S(2)}) %collective-permute-start.3) | collective-permute-done | bytes 196640 | tf_op jit(solution)/shard_map/ppermute | solution.py:476
  57.3 4.9 %all-to-all-start.1 = ((bf16[32,16,256]{2,1,0:T(8,128)(2,1)}), bf16[32,16,256]{2,1,0:T(8,128)(2,1)}, u32[]{:S(2)}, u32[]{:S(2)}) async-start(bf16[32,16,256]{2,1,0:T(8,128)(2,1)} %bitcast.12), calls=%async_computation.1 | async-start | bytes 524288 | tf_op jit(solution)/shard_map/all_to_all | solution.py:492
  62.2 11.3 %all-to-all-done.1 = bf16[32,16,256]{2,1,0:T(8,128)(2,1)} async-done(((bf16[32,16,256]{2,1,0:T(8,128)(2,1)}), bf16[32,16,256]{2,1,0:T(8,128)(2,1)}, u32[]{:S(2)}, u32[]{:S(2)}) %all-to-all-start.1) | async-done | bytes 262176 | tf_op jit(solution)/shard_map/all_to_all | solution.py:492
  73.5 5.1 %lines_in.1 = (f32[2,2,192,128]{3,2,1,0:T(8,128)}, f32[32,128]{1,0:T(8,128)}) custom-call(bf16[512,256]{1,0:T(8,128)(2,1)} %bitcast.4.back_hbm, bf16[2,384,512]{2,1,0:T(8,128)(2,1)} %constant.42.clone.table_hbm, f32[2,2,192,128]{3,2,1,0:T(8,128)} %bitcast.11, f32[8,2,192,128]{3,2,1,0:T(8,128)} %beta_hbm.3, f32[32,128]{1,0:T(8,128)} %get-tuple-element.21.mixed_ref, ...), custom_call_target="tpu_custom_call" | custom-call | tf_op jit(solution)/shard_map/lines_in/pallas_call | solution.py:585
  78.6 3.7 %all-to-all-start.2 = ((f32[32,1,128]{2,1,0:T(1,128)}), f32[32,1,128]{2,1,0:T(1,128)S(1)}, u32[]{:S(2)}, u32[]{:S(2)}) async-start(f32[32,1,128]{2,1,0:T(1,128)} %bitcast.15), calls=%async_computation.2 | async-start | bytes 32768 | tf_op jit(solution)/shard_map/all_to_all | solution.py:492
  82.3 0.7 compare_and_fusion
  83.0 6.7 %all-to-all-done.2 = f32[32,1,128]{2,1,0:T(1,128)S(1)} async-done(((f32[32,1,128]{2,1,0:T(1,128)}), f32[32,1,128]{2,1,0:T(1,128)S(1)}, u32[]{:S(2)}, u32[]{:S(2)}) %all-to-all-start.2) | async-done | bytes 16416 | tf_op jit(solution)/shard_map/all_to_all | solution.py:492
  89.7 0.1 mul.18
  89.8 0.1 broadcast_select_fusion
  89.9 0.7 copy.20
  (2 shorter events, 0.0 us)
Async XLA Ops:
  25.4 30.2 %collective-permute-start = (bf16[2,2,192,128]{3,2,1,0:T(8,128)(2,1)}, bf16[2,2,192,128]{3,2,1,0:T(8,128)(2,1)}, u32[]{:S(2)}, u32[]{:S(2)}) collective-permute-start(bf16[2,2,192,128]{3,2,1,0:T(8,128)(2,1)} %get-tuple-element.19), channel_id=1, source_target_pairs={{0,64},{32,96},{64,128},{96,160},{128,192},{160,224},{192,0},{224,... | collective-permute-start | bytes 589832 | tf_op jit(solution)/shard_map/ppermute | solution.py:476
  29.5 26.0 %collective-permute-start.1 = (bf16[2,2,192,128]{3,2,1,0:T(8,128)(2,1)}, bf16[2,2,192,128]{3,2,1,0:T(8,128)(2,1)}, u32[]{:S(2)}, u32[]{:S(2)}) collective-permute-start(bf16[2,2,192,128]{3,2,1,0:T(8,128)(2,1)} %get-tuple-element.19), channel_id=1, source_target_pairs={{0,32},{32,64},{64,96},{96,128},{128,160},{160,192},{192,224},{224... | collective-permute-start | bytes 589832 | tf_op jit(solution)/shard_map/ppermute | solution.py:476
  31.3 24.2 %collective-permute-start.2 = (bf16[2,2,192,128]{3,2,1,0:T(8,128)(2,1)}, bf16[2,2,192,128]{3,2,1,0:T(8,128)(2,1)}, u32[]{:S(2)}, u32[]{:S(2)}) collective-permute-start(bf16[2,2,192,128]{3,2,1,0:T(8,128)(2,1)} %get-tuple-element.19), channel_id=1, source_target_pairs={{0,224},{32,0},{64,32},{96,64},{128,96},{160,128},{192,160},{224,1... | collective-permute-start | bytes 589832 | tf_op jit(solution)/shard_map/ppermute | solution.py:476
  31.3 26.0 %collective-permute-start.3 = (bf16[2,2,192,128]{3,2,1,0:T(8,128)(2,1)}, bf16[2,2,192,128]{3,2,1,0:T(8,128)(2,1)}, u32[]{:S(2)}, u32[]{:S(2)}) collective-permute-start(bf16[2,2,192,128]{3,2,1,0:T(8,128)(2,1)} %get-tuple-element.19), channel_id=1, source_target_pairs={{0,192},{32,224},{64,0},{96,32},{128,64},{160,96},{192,128},{224,1... | collective-permute-start | bytes 589832 | tf_op jit(solution)/shard_map/ppermute | solution.py:476
  57.3 16.2 %all-to-all-start.1 = ((bf16[32,16,256]{2,1,0:T(8,128)(2,1)}), bf16[32,16,256]{2,1,0:T(8,128)(2,1)}, u32[]{:S(2)}, u32[]{:S(2)}) async-start(bf16[32,16,256]{2,1,0:T(8,128)(2,1)} %bitcast.12), calls=%async_computation.1 | async-start | bytes 524288 | tf_op jit(solution)/shard_map/all_to_all | solution.py:492
  78.6 11.1 %all-to-all-start.2 = ((f32[32,1,128]{2,1,0:T(1,128)}), f32[32,1,128]{2,1,0:T(1,128)S(1)}, u32[]{:S(2)}, u32[]{:S(2)}) async-start(f32[32,1,128]{2,1,0:T(1,128)} %bitcast.15), calls=%async_computation.2 | async-start | bytes 32768 | tf_op jit(solution)/shard_map/all_to_all | solution.py:492

commit v4 on v3

--- a/solution.py
+++ b/solution.py
@@ -22,6 +22,7 @@
 LANES = 128
 WIDTH = LANES // GROUPS
 STEP = LANES + 1
+OFFSETS = (-2, -1, 1, 2)
 BF = jnp.bfloat16
 F32 = jnp.float32
 HIGHEST = lax.Precision.HIGHEST
@@ -32,6 +33,15 @@
     angle = (index[:, None] * index[None, :] % GRID) * (2.0 * math.pi / GRID)
     factor = 1.0 / math.sqrt(GRID)
     return np.cos(angle) * factor, np.sin(angle) * factor
+
+
+def rounded(exact):
+    return np.asarray(exact).astype(jnp.bfloat16).astype(np.float64)
+
+
+def side_by_side(exact):
+    high = rounded(exact)
+    return np.concatenate([high, exact - high], axis=1)
 
 
 def build_tables():
@@ -77,17 +87,18 @@
                         mix_out[part + other + DEPTH, im] = turn.real
                 fold[b * ROWS + zi, re] = 1.0
                 fold[b * ROWS + DEPTH + zi, im] = 1.0
-    x_inverse = np.zeros((GROUPS, 2 * SPAN, 2 * SPAN))
-    x_forward = np.zeros((GROUPS, 2 * SPAN, 2 * SPAN))
+    balance = 1.6242 / 16.0 * math.sqrt(GRID)
+    x_inverse = np.zeros((GROUPS, 2 * SPAN, 4 * SPAN))
+    x_forward = np.zeros((GROUPS, 2 * SPAN, 4 * SPAN))
     for g in range(GROUPS):
-        c, s = cos[:SPAN, g::GROUPS], sin[:SPAN, g::GROUPS]
-        x_inverse[g] = np.block([[c.T, -s.T], [s.T, c.T]])
-        x_forward[g] = np.block([[c, s], [-s, c]])
+        c, s = cos[:SPAN, g::GROUPS] / balance, sin[:SPAN, g::GROUPS] / balance
+        x_inverse[g] = side_by_side(np.block([[c.T, -s.T], [s.T, c.T]]))
+        x_forward[g] = side_by_side(np.block([[c, s], [-s, c]]))
     return dict(
         to_planes=to_planes,
         from_planes=from_planes,
         spread=spread,
-        y_table=np.concatenate([cos, sin], axis=0),
+        y_table=np.concatenate([cos, sin], axis=0) * balance,
         mix_in=mix_in,
         mix_out=mix_out,
         x_inverse=x_inverse,
@@ -118,13 +129,22 @@
     return copy
 
 
+def lane_sums(rows):
+    count = rows.shape[0]
+    total = jnp.sum(rows, axis=1, keepdims=True)
+    row = lax.broadcasted_iota(jnp.int32, (count, LANES), 0)
+    lane = lax.broadcasted_iota(jnp.int32, (count, LANES), 1)
+    return jnp.sum(jnp.where(row == lane, total, 0.0), axis=0, keepdims=True)
+
+
 def send_kernel(
     block_hbm,
     beta_hbm,
-    columns_ref,
+    columns_hbm,
     table_hbm,
     send_hbm,
     low_hbm,
+    columns_ref,
     block_ref,
     beta_ref,
     table_ref,
@@ -133,6 +153,7 @@
     sems,
 ):
     block_copy = load(block_hbm, block_ref, sems.at[0])
+    columns_copy = load(columns_hbm, columns_ref, sems.at[10])
     table_copy = load(table_hbm, table_ref, sems.at[1])
     beta_copies = [load(beta_hbm.at[j], beta_ref.at[j], sems.at[2 + j]) for j in range(PROJ)]
     block_copy.wait()
@@ -143,8 +164,6 @@
     )
     wave_high = wave.astype(BF)
     wave_low = (wave - wave_high.astype(F32)).astype(BF)
-    table_copy.wait()
-    lines = dot(table_ref[0], wave_high) + (dot(table_ref[1], wave_high) + dot(table_ref[0], wave_low))
     sums = [None] * (BANDS * PROJ * 2)
     for j in range(PROJ):
         beta_copies[j].wait()
@@ -154,21 +173,32 @@
             at = (b * PROJ + j) * 2
             sums[at] = jnp.sum(br * wr + bi * wi, axis=0, keepdims=True)
             sums[at + 1] = jnp.sum(br * wi - bi * wr, axis=0, keepdims=True)
-    stacked = jnp.concatenate(sums, axis=0)
-    spread = jnp.concatenate([stacked, jnp.zeros((LANES - 32, LANES), F32)], axis=0)
-    total = dot_nt(jnp.ones((8, LANES), F32), spread, HIGHEST)[0:1]
+    total = lane_sums(jnp.concatenate(sums, axis=0))
     high = total.astype(BF).astype(F32)
     middle = (total - high).astype(BF).astype(F32)
     low = total - high - middle
+    columns_copy.wait()
     cols = columns_ref[...]
     col_x = cols // GRID
     first = jnp.concatenate([col_x, cols - col_x * GRID], axis=1).astype(F32)
     other = jnp.concatenate([high, middle, low], axis=0)
     other = jnp.concatenate([other, jnp.zeros((3, LANES), F32)], axis=1)
     meta = jnp.concatenate([jnp.zeros((2 * DEPTH, 2 * LANES), F32), first, other], axis=0)
-    lines = lines.reshape(PW, ROWS, 2 * LANES) + meta[None]
-    lines_ref[...] = lines.astype(BF)
-    load(lines_ref, send_hbm, sems.at[10]).wait()
+    table_copy.wait()
+    outs = []
+    some = PW // 4
+    for start in range(0, PW, some):
+        part = slice(start * ROWS, (start + some) * ROWS)
+        high_table = table_ref[0, part, :]
+        lines = dot(high_table, wave_high) + (
+            dot(table_ref[1, part, :], wave_high) + dot(high_table, wave_low)
+        )
+        lines = lines.reshape(some, ROWS, 2 * LANES) + meta[None]
+        lines_ref[start : start + some] = lines.astype(BF)
+        piece = pl.ds(start, some)
+        outs.append(load(lines_ref.at[piece], send_hbm.at[piece], sems.at[12 + start // some]))
+    for copy in outs:
+        copy.wait()
     low_copy.wait()
 
 
@@ -182,8 +212,10 @@
     x_inv_hbm,
     x_fwd_hbm,
     fold_hbm,
+    coupling_hbm,
+    back_hbm,
+    mixed_hbm,
     coupling_ref,
-    back_hbm,
     mixed_ref,
     recv_ref,
     pot_ref,
@@ -220,6 +252,7 @@
         (pot_hbm, pot_ref),
     )
     copies = [load(a, b, sems.at[k]) for k, (a, b) in enumerate(pairs)]
+    coupling_copy = load(coupling_hbm, coupling_ref, sems.at[14])
 
     def clear(i, _):
         grid_ref[pl.ds(pl.multiple_of(i * 256, 256), 256), :] = jnp.zeros((256, LANES), F32)
@@ -249,10 +282,12 @@
     row = lax.broadcasted_iota(jnp.int32, (32, PROJ), 0)
     column = lax.broadcasted_iota(jnp.int32, (32, PROJ), 1)
     widen = (row // 2 % PROJ == column).astype(F32)
+    coupling_copy.wait()
     coupling = coupling_ref[...]
     couple = dot_nt(dot(widen, 0.5 * (coupling + coupling.T), HIGHEST), widen, HIGHEST)
     couple = jnp.where(same, couple * (1.0 / math.sqrt(COLS * GRID)), 0.0)
     mixed_ref[...] = dot(couple, sums, HIGHEST)
+    mixed_copy = load(mixed_ref, mixed_hbm, sems.at[14])
     turned = turned.astype(BF)
     for s in range(8):
         for g in range(PW // 8):
@@ -330,8 +365,9 @@
                     ],
                     axis=1,
                 ).astype(BF)
-                field = (dot(x_inv_ref[g], plane) * pot).astype(BF)
-                back = dot(x_fwd_ref[g], field)
+                field = dot(x_inv_ref[g], jnp.concatenate([plane, plane], axis=0))
+                field = (field * pot).astype(BF)
+                back = dot(x_fwd_ref[g], jnp.concatenate([field, field], axis=0))
                 for ri, place in enumerate(places):
                     near_out_ref[place, :] = back[ri * SPAN : (ri + 1) * SPAN, :LANES]
                     far_out_ref[place, :] = back[ri * SPAN : (ri + 1) * SPAN, LANES:]
@@ -369,6 +405,7 @@
     lax.fori_loop(0, PW, gather, 0)
 
     outs = []
+    outs.append(mixed_copy)
     for d in range(PW):
         part = slice(d * LANES, (d + 1) * LANES)
         kept = (rows_ref[part, :] * mask_ref[part, :]).astype(BF)
@@ -387,13 +424,16 @@
     table_hbm,
     block_hbm,
     beta_hbm,
-    mixed_ref,
-    columns_ref,
+    mixed_hbm,
+    columns_hbm,
     other_0,
     other_1,
     other_2,
     other_3,
     applied_hbm,
+    cross_hbm,
+    mixed_ref,
+    columns_ref,
     cross_ref,
     back_ref,
     table_ref,
@@ -404,32 +444,44 @@
     applied_ref,
     sems,
 ):
-    pairs = (
-        (back_hbm, back_ref),
-        (table_hbm, table_ref),
-        (block_hbm, block_ref),
-        (beta_hbm, beta_ref),
-        (other_0, others_ref.at[0]),
-        (other_1, others_ref.at[1]),
-        (other_2, others_ref.at[2]),
-        (other_3, others_ref.at[3]),
-    )
-    copies = [load(a, b, sems.at[k]) for k, (a, b) in enumerate(pairs)]
+    chunk = 48
+    steps = range(0, GRID, chunk)
+    back_copy = load(back_hbm, back_ref, sems.at[0])
+    table_copy = load(table_hbm, table_ref, sems.at[1])
+    columns_copy = load(columns_hbm, columns_ref, sems.at[18])
+    mixed_copy = load(mixed_hbm, mixed_ref, sems.at[19])
+
+    def load_chunk(k):
+        part = pl.ds(k * chunk, chunk)
+        return (
+            load(block_hbm.at[:, :, part], block_ref.at[:, :, part], sems.at[6 + 2 * k]),
+            load(beta_hbm.at[:, :, part], beta_ref.at[:, :, part], sems.at[7 + 2 * k]),
+        )
+
+    chunk_copies = [load_chunk(0)]
+    other_copies = [
+        load(other, others_ref.at[o], sems.at[2 + o])
+        for o, other in enumerate((other_0, other_1, other_2, other_3))
+    ]
+    chunk_copies += [load_chunk(k) for k in range(1, len(steps))]
+    band = lax.axis_index("band")
+    bands = lax.axis_size("band")
+    columns_copy.wait()
+    mixed_copy.wait()
     cols = columns_ref[...]
     col_x = cols // GRID
     fx = wrapped(col_x)
     fy = wrapped(cols - col_x * GRID)
     fxy = fx * fx + fy * fy
-    copies[0].wait()
-    copies[1].wait()
+    back_copy.wait()
+    table_copy.wait()
     local_ref[...] = dot(table_ref[0], back_ref[...]) + dot(table_ref[1], back_ref[...])
-    for copy in copies[2:]:
-        copy.wait()
-    chunk = 48
     totals = [jnp.zeros((8, LANES), F32) for _ in range(32)]
     outs = []
-    for start in range(0, GRID, chunk):
+    for k, start in enumerate(steps):
         part = slice(start, start + chunk)
+        for copy in chunk_copies[k]:
+            copy.wait()
         fz = wrapped(lax.broadcasted_iota(jnp.int32, (chunk, LANES), 0) + start)
         kinetic = (fz * fz + fxy).astype(F32) * (4.0 / (GRID * GRID))
         low = []
@@ -438,10 +490,10 @@
             imag = local_ref[GRID + start : GRID + start + chunk, b * LANES : (b + 1) * LANES]
             real = real + kinetic * block_ref[b, 0, part]
             imag = imag + kinetic * block_ref[b, 1, part]
-            for k in range(PROJ):
-                at = (b * PROJ + k) * 2
+            for j in range(PROJ):
+                at = (b * PROJ + j) * 2
                 mr, mi = mixed_ref[at : at + 1, :], mixed_ref[at + 1 : at + 2, :]
-                br, bi = beta_ref[k, 0, part], beta_ref[k, 1, part]
+                br, bi = beta_ref[j, 0, part], beta_ref[j, 1, part]
                 real = real + mr * br - mi * bi
                 imag = imag + mr * bi + mi * br
             applied_ref[b, 0, part] = real
@@ -451,9 +503,12 @@
             load(
                 applied_ref.at[:, :, pl.ds(start, chunk)],
                 applied_hbm.at[:, :, pl.ds(start, chunk)],
-                sems.at[8 + start // chunk],
+                sems.at[14 + k],
             )
         )
+        if k == 0:
+            for copy in other_copies:
+                copy.wait()
         for o in range(4):
             for m in range(BANDS):
                 otr = others_ref[o, m, 0, part].astype(F32)
@@ -464,9 +519,15 @@
                     imag = (otr * ai - oti * ar).reshape(chunk // 8, 8, LANES).sum(0)
                     totals[o * 8 + m * 2 + n] += real
                     totals[o * 8 + 4 + m * 2 + n] += imag
-    stacked = jnp.concatenate([jnp.sum(t, axis=0, keepdims=True) for t in totals], axis=0)
-    spread = jnp.concatenate([stacked, jnp.zeros((LANES - 32, LANES), F32)], axis=0)
-    cross_ref[...] = dot_nt(jnp.ones((PW, LANES), F32), spread, HIGHEST)
+    scale = 1.0 / math.sqrt(COLS * GRID)
+    rows = []
+    for o, offset in enumerate(OFFSETS):
+        inside = (band + offset >= 0) & (band + offset < bands)
+        factor = jnp.where(inside, scale, 0.0)
+        rows += [jnp.sum(t, axis=0, keepdims=True) * factor for t in totals[o * 8 : o * 8 + 8]]
+    sums = lane_sums(jnp.concatenate(rows, axis=0))
+    cross_ref[...] = jnp.zeros((PW, LANES), F32) + sums
+    outs.append(load(cross_ref, cross_hbm, sems.at[18]))
     for copy in outs:
         copy.wait()
 
@@ -476,16 +537,8 @@
     return lax.ppermute(value, axis, [(s, (s + steps) % count) for s in range(count)])
 
 
-def vmem():
-    return pl.BlockSpec(memory_space=pltpu.VMEM)
-
-
 def hbm():
     return pl.BlockSpec(memory_space=pltpu.HBM)
-
-
-def smem():
-    return pl.BlockSpec(memory_space=pltpu.SMEM)
 
 
 def exchange(value):
@@ -500,9 +553,11 @@
             jax.ShapeDtypeStruct((PW * ROWS, 2 * LANES), BF),
             jax.ShapeDtypeStruct((32, LANES), F32),
         ),
-        in_specs=[hbm()] * 9 + [vmem()],
-        out_specs=(hbm(), vmem()),
+        in_specs=[hbm()] * 10,
+        out_specs=(hbm(), hbm()),
         scratch_shapes=[
+            pltpu.VMEM((PROJ, PROJ), F32),
+            pltpu.VMEM((32, LANES), F32),
             pltpu.VMEM((PW * ROWS, 2 * LANES), BF),
             pltpu.VMEM((DEPTH, GRID, GRID), F32),
         ]
@@ -523,7 +578,7 @@
             pltpu.VMEM((DEPTH * GRID, LANES), F32),
             pltpu.VMEM((PW, LOCAL), jnp.int32),
             pltpu.SMEM((PW, LOCAL), jnp.int32),
-            pltpu.SemaphoreType.DMA((14,)),
+            pltpu.SemaphoreType.DMA((15,)),
         ],
         compiler_params=pltpu.CompilerParams(vmem_limit_bytes=64 << 20),
         cost_estimate=pl.CostEstimate(
@@ -544,7 +599,7 @@
 
 
 def two_parts(exact):
-    high = np.asarray(exact).astype(jnp.bfloat16).astype(np.float64)
+    high = rounded(exact)
     return jnp.asarray(np.stack([high, exact - high]), BF)
 
 
@@ -553,7 +608,6 @@
     half = {k: jnp.asarray(v, BF) for k, v in tables.items()}
     block = orbitals[0]
     own_columns = columns.reshape(1, LOCAL)
-    scale = 1.0 / math.sqrt(COLS * GRID)
     sent, low_orbitals = pl.pallas_call(
         send_kernel,
         name="lines_out",
@@ -561,22 +615,22 @@
             jax.ShapeDtypeStruct((PW, ROWS, 2 * LANES), BF),
             jax.ShapeDtypeStruct((BANDS, 2, GRID, LOCAL), BF),
         ),
-        in_specs=[hbm(), hbm(), vmem(), hbm()],
+        in_specs=[hbm()] * 4,
         out_specs=(hbm(), hbm()),
         scratch_shapes=[
+            pltpu.VMEM((1, LOCAL), jnp.int32),
             pltpu.VMEM((BANDS, 2, GRID, LOCAL), F32),
             pltpu.VMEM((PROJ, 2, GRID, LOCAL), F32),
             pltpu.VMEM((2, PW * ROWS, 2 * GRID), BF),
             pltpu.VMEM((PW, ROWS, 2 * LANES), BF),
             pltpu.VMEM((BANDS, 2, GRID, LOCAL), BF),
-            pltpu.SemaphoreType.DMA((12,)),
+            pltpu.SemaphoreType.DMA((16,)),
         ],
         compiler_params=pltpu.CompilerParams(vmem_limit_bytes=64 << 20),
     )(block, projectors, own_columns, two_parts(tables["to_planes"]))
     recv = exchange(sent)
     recv, low_orbitals = lax.optimization_barrier((recv, low_orbitals))
-    offsets = (-2, -1, 1, 2)
-    others = [around(low_orbitals, "band", -offset) for offset in offsets]
+    others = [around(low_orbitals, "band", -offset) for offset in OFFSETS]
 
     back, mixed = planes_call(recv.reshape(PW * ROWS, 2 * LANES), potential, half, coupling)
     back, others = lax.optimization_barrier((back, others))
@@ -589,9 +643,12 @@
             jax.ShapeDtypeStruct((BANDS, 2, GRID, LOCAL), F32),
             jax.ShapeDtypeStruct((PW, LANES), F32),
         ),
-        in_specs=[hbm()] * 4 + [vmem()] * 2 + [hbm()] * 4,
-        out_specs=(hbm(), vmem()),
+        in_specs=[hbm()] * 10,
+        out_specs=(hbm(), hbm()),
         scratch_shapes=[
+            pltpu.VMEM((32, LANES), F32),
+            pltpu.VMEM((1, LOCAL), jnp.int32),
+            pltpu.VMEM((PW, LANES), F32),
             pltpu.VMEM((PW * ROWS, 2 * LANES), BF),
             pltpu.VMEM((2, 2 * GRID, PW * ROWS), BF),
             pltpu.VMEM((BANDS, 2, GRID, LOCAL), F32),
@@ -599,7 +656,7 @@
             pltpu.VMEM((4, BANDS, 2, GRID, LOCAL), BF),
             pltpu.VMEM((2 * GRID, 2 * LANES), F32),
             pltpu.VMEM((BANDS, 2, GRID, LOCAL), F32),
-            pltpu.SemaphoreType.DMA((12,)),
+            pltpu.SemaphoreType.DMA((20,)),
         ],
         compiler_params=pltpu.CompilerParams(vmem_limit_bytes=64 << 20),
     )(
@@ -612,10 +669,7 @@
         *others,
     )
     every = exchange(cross)
-    summed = jnp.sum(every[:, :32], axis=0).reshape(4, 2, BANDS, BANDS)
-    source = lax.axis_index("band") + np.asarray(offsets, np.int32)
-    inside = (source >= 0) & (source < lax.axis_size("band"))
-    cross_terms = jnp.where(inside[:, None, None, None], summed * scale, 0.0)
+    cross_terms = jnp.sum(every[:, :32], axis=0).reshape(4, 2, BANDS, BANDS)
     return applied[None], cross_terms[None]
 
 

time: 91.1 us -> 88.6 us (0.973)
  the two profiles are of different devices: /device:TPU:5 before, /device:TPU:3 now
where the time goes in v4:
time: 88.6 us; the launch traced here: 88.2 us
  blocking collectives  47.9 us (54%)
  Pallas kernels  25.8 us (29%)
  starting transfers between devices  10.5 us (12%)
  waiting for transfers between devices  2.5 us (3%)
    all_to_all x3, blocking collectives, exchange(): return lax.all_to_all(value, 'pw', split_axis=0, concat_axis=0, tiled=True)  47.9 us
    pallas_call x1, Pallas kernels, planes_call(): pl.pallas_call(planes_kernel, name=name, out_shape=(jax.ShapeDtypeStruct(...  18.8 us
    ppermute x4, starting transfers between devices, around(): lax.ppermute(value, axis, [(s, (s + steps) % count) for s in range(count)])  10.5 us
    pallas_call x1, Pallas kernels, per_device(): pl.pallas_call(finish_kernel, name='lines_in', out_shape=(jax.ShapeDtypeS...  3.58 us
    pallas_call x1, Pallas kernels, per_device(): pl.pallas_call(send_kernel, name='lines_out', out_shape=(jax.ShapeDtypeSt...  3.42 us
    ppermute x4, waiting for transfers between devices, around(): lax.ppermute(value, axis, [(s, (s + steps) % count) for s in range(count)])  2.5 us
  transfers between devices with their start and end apart: 4, of which 1 were waited for; matrix products, arithmetic and copies ran while one was open for 0% of the time, Pallas kernels for 21%

profile of v4, /device:TPU:3, one launch (start us, length us, event | category | flops | bytes accessed | tf_op | source)
XLA Modules:
  0.0 88.2 jit_solution(14588702665466900672)
XLA Ops:
  0.6 3.4 %lines_out.1 = (bf16[32,16,256]{2,1,0:T(8,128)(2,1)}, bf16[2,2,192,128]{3,2,1,0:T(8,128)(2,1)}) custom-call(f32[2,2,192,128]{3,2,1,0:T(8,128)} %bitcast.10, f32[8,2,192,128]{3,2,1,0:T(8,128)} %beta_hbm.3, s32[1,128]{1,0:T(1,128)} %bitcast.17, bf16[2,512,384]{2,1,0:T(8,128)(2,1)} %constant.27.clone.table_hbm), custom_call_target="tpu_custom_call" | custom-call | tf_op jit(solution)/shard_map/lines_out/pallas_call | solution.py:611
  4.1 20.6 %all_to_all.22 = bf16[32,16,256]{2,1,0:T(8,128)(2,1)} all-to-all(bf16[32,16,256]{2,1,0:T(8,128)(2,1)} %get-tuple-element.15), channel_id=1, replica_groups=mesh['band'=8,'pw'=32] {'pw'}, dimensions={0} | all-to-all | bytes 524288 | tf_op jit(solution)/shard_map/all_to_all | solution.py:545
  24.6 5.8 %collective-permute-start.3 = (bf16[2,2,192,128]{3,2,1,0:T(8,128)(2,1)}, bf16[2,2,192,128]{3,2,1,0:T(8,128)(2,1)}, u32[]{:S(2)}, u32[]{:S(2)}) collective-permute-start(bf16[2,2,192,128]{3,2,1,0:T(8,128)(2,1)} %get-tuple-element.19), channel_id=1, source_target_pairs={{0,192},{32,224},{64,0},{96,32},{128,64},{160,96},{192,128},{224,1... | collective-permute-start | bytes 589832 | tf_op jit(solution)/shard_map/ppermute | solution.py:537
  30.4 1.2 %collective-permute-start.2 = (bf16[2,2,192,128]{3,2,1,0:T(8,128)(2,1)}, bf16[2,2,192,128]{3,2,1,0:T(8,128)(2,1)}, u32[]{:S(2)}, u32[]{:S(2)}) collective-permute-start(bf16[2,2,192,128]{3,2,1,0:T(8,128)(2,1)} %get-tuple-element.19), channel_id=1, source_target_pairs={{0,224},{32,0},{64,32},{96,64},{128,96},{160,128},{192,160},{224,1... | collective-permute-start | bytes 589832 | tf_op jit(solution)/shard_map/ppermute | solution.py:537
  31.6 0.3 collective-permute-start.1
  31.9 3.2 %collective-permute-start = (bf16[2,2,192,128]{3,2,1,0:T(8,128)(2,1)}, bf16[2,2,192,128]{3,2,1,0:T(8,128)(2,1)}, u32[]{:S(2)}, u32[]{:S(2)}) collective-permute-start(bf16[2,2,192,128]{3,2,1,0:T(8,128)(2,1)} %get-tuple-element.19), channel_id=1, source_target_pairs={{0,64},{32,96},{64,128},{96,160},{128,192},{160,224},{192,0},{224,... | collective-permute-start | bytes 589832 | tf_op jit(solution)/shard_map/ppermute | solution.py:537
  35.1 18.8 %planes.1 = (bf16[512,256]{1,0:T(8,128)(2,1)}, f32[32,128]{1,0:T(8,128)}) custom-call(bf16[512,256]{1,0:T(8,128)(2,1)} %bitcast.13, f32[6,192,192]{2,1,0:T(8,128)} %pot_hbm.1, bf16[8,256,256]{2,1,0:T(8,128)(2,1)} %constant.20.clone.spread_hbm, bf16[384,192]{1,0:T(8,128)(2,1)} %constant.21.clone.y_hbm, bf16[128,256]{1,0:T(8,128)(2,1)} %constant.22.clone.mix_in_hbm, ...), custom_call_target="tpu_custom_call" | custom-call | flops 20000000000 | bytes 4194304 | tf_op jit(solution)/shard_map/planes/pallas_call | solution.py:549
  53.9 0.0 collective-permute-done.3.other_3
  53.9 0.0 collective-permute-done.2.other_2
  53.9 0.0 collective-permute-done.1.other_1
  53.9 2.5 %collective-permute-done.other_0 = bf16[2,2,192,128]{3,2,1,0:T(8,128)(2,1)} collective-permute-done((bf16[2,2,192,128]{3,2,1,0:T(8,128)(2,1)}, bf16[2,2,192,128]{3,2,1,0:T(8,128)(2,1)}, u32[]{:S(2)}, u32[]{:S(2)}) %collective-permute-start) | collective-permute-done | bytes 196640 | tf_op jit(solution)/shard_map/ppermute | solution.py:537
  56.4 16.2 %all_to_all.23 = bf16[32,16,256]{2,1,0:T(8,128)(2,1)} all-to-all(bf16[32,16,256]{2,1,0:T(8,128)(2,1)} %bitcast.14), channel_id=1, replica_groups=mesh['band'=8,'pw'=32] {'pw'}, dimensions={0} | all-to-all | bytes 524288 | tf_op jit(solution)/shard_map/all_to_all | solution.py:545
  72.6 3.6 %lines_in.1 = (f32[2,2,192,128]{3,2,1,0:T(8,128)}, f32[32,128]{1,0:T(8,128)}) custom-call(bf16[512,256]{1,0:T(8,128)(2,1)} %bitcast.12, bf16[2,384,512]{2,1,0:T(8,128)(2,1)} %constant.28.clone.table_hbm, f32[2,2,192,128]{3,2,1,0:T(8,128)} %bitcast.11, f32[8,2,192,128]{3,2,1,0:T(8,128)} %beta_hbm.3, f32[32,128]{1,0:T(8,128)} %get-tuple-element.21.mixed_hbm, ...), custom_call_target="tpu_custom_call" | custom-call | tf_op jit(solution)/shard_map/lines_in/pallas_call | solution.py:639
  76.2 11.1 %all_to_all.24 = f32[32,1,128]{2,1,0:T(1,128)S(1)} all-to-all(f32[32,1,128]{2,1,0:T(1,128)} %bitcast.16), channel_id=1, replica_groups=mesh['band'=8,'pw'=32] {'pw'}, dimensions={0} | all-to-all | bytes 32768 | tf_op jit(solution)/shard_map/all_to_all | solution.py:545
  87.3 0.1 broadcast_in_dim_reshape.3
  87.4 0.7 copy.19
  (1 shorter events, 0.0 us)
Async XLA Ops:
  24.6 29.3 %collective-permute-start.3 = (bf16[2,2,192,128]{3,2,1,0:T(8,128)(2,1)}, bf16[2,2,192,128]{3,2,1,0:T(8,128)(2,1)}, u32[]{:S(2)}, u32[]{:S(2)}) collective-permute-start(bf16[2,2,192,128]{3,2,1,0:T(8,128)(2,1)} %get-tuple-element.19), channel_id=1, source_target_pairs={{0,192},{32,224},{64,0},{96,32},{128,64},{160,96},{192,128},{224,1... | collective-permute-start | bytes 589832 | tf_op jit(solution)/shard_map/ppermute | solution.py:537
  30.4 23.5 %collective-permute-start.2 = (bf16[2,2,192,128]{3,2,1,0:T(8,128)(2,1)}, bf16[2,2,192,128]{3,2,1,0:T(8,128)(2,1)}, u32[]{:S(2)}, u32[]{:S(2)}) collective-permute-start(bf16[2,2,192,128]{3,2,1,0:T(8,128)(2,1)} %get-tuple-element.19), channel_id=1, source_target_pairs={{0,224},{32,0},{64,32},{96,64},{128,96},{160,128},{192,160},{224,1... | collective-permute-start | bytes 589832 | tf_op jit(solution)/shard_map/ppermute | solution.py:537
  31.6 22.4 %collective-permute-start.1 = (bf16[2,2,192,128]{3,2,1,0:T(8,128)(2,1)}, bf16[2,2,192,128]{3,2,1,0:T(8,128)(2,1)}, u32[]{:S(2)}, u32[]{:S(2)}) collective-permute-start(bf16[2,2,192,128]{3,2,1,0:T(8,128)(2,1)} %get-tuple-element.19), channel_id=1, source_target_pairs={{0,32},{32,64},{64,96},{96,128},{128,160},{160,192},{192,224},{224... | collective-permute-start | bytes 589832 | tf_op jit(solution)/shard_map/ppermute | solution.py:537
  31.9 24.6 %collective-permute-start = (bf16[2,2,192,128]{3,2,1,0:T(8,128)(2,1)}, bf16[2,2,192,128]{3,2,1,0:T(8,128)(2,1)}, u32[]{:S(2)}, u32[]{:S(2)}) collective-permute-start(bf16[2,2,192,128]{3,2,1,0:T(8,128)(2,1)} %get-tuple-element.19), channel_id=1, source_target_pairs={{0,64},{32,96},{64,128},{96,160},{128,192},{160,224},{192,0},{224,... | collective-permute-start | bytes 589832 | tf_op jit(solution)/shard_map/ppermute | solution.py:537

commit v5 on v4

--- a/solution.py
+++ b/solution.py
@@ -629,7 +629,6 @@
         compiler_params=pltpu.CompilerParams(vmem_limit_bytes=64 << 20),
     )(block, projectors, own_columns, two_parts(tables["to_planes"]))
     recv = exchange(sent)
-    recv, low_orbitals = lax.optimization_barrier((recv, low_orbitals))
     others = [around(low_orbitals, "band", -offset) for offset in OFFSETS]
 
     back, mixed = planes_call(recv.reshape(PW * ROWS, 2 * LANES), potential, half, coupling)

time: 88.6 us -> 84.9 us (0.958)
  the two profiles are of different devices: /device:TPU:3 before, /device:TPU:129 now
where the time goes in v5:
time: 84.9 us; the launch traced here: 84.6 us
  blocking collectives  26.7 us (31%)
  Pallas kernels  25.8 us (30%)
  waiting for transfers between devices  18 us (21%)
  starting transfers between devices  12.5 us (15%)
    all_to_all x2, blocking collectives, exchange(): return lax.all_to_all(value, 'pw', split_axis=0, concat_axis=0, tiled=True)  26.7 us
    pallas_call x1, Pallas kernels, planes_call(): pl.pallas_call(planes_kernel, name=name, out_shape=(jax.ShapeDtypeStruct(...  18.8 us
    all_to_all x1, waiting for transfers between devices, exchange(): return lax.all_to_all(value, 'pw', split_axis=0, concat_axis=0, tiled=True)  18 us
    all_to_all x1, starting transfers between devices, exchange(): return lax.all_to_all(value, 'pw', split_axis=0, concat_axis=0, tiled=True)  6.73 us
    ppermute x4, starting transfers between devices, around(): lax.ppermute(value, axis, [(s, (s + steps) % count) for s in range(count)])  5.8 us
    pallas_call x1, Pallas kernels, per_device(): pl.pallas_call(finish_kernel, name='lines_in', out_shape=(jax.ShapeDtypeS...  3.58 us
    pallas_call x1, Pallas kernels, per_device(): pl.pallas_call(send_kernel, name='lines_out', out_shape=(jax.ShapeDtypeSt...  3.42 us
  transfers between devices with their start and end apart: 5, of which 1 were waited for; matrix products, arithmetic and copies ran while one was open for 0% of the time, Pallas kernels for 22%

profile of v5, /device:TPU:129, one launch (start us, length us, event | category | flops | bytes accessed | tf_op | source)
XLA Modules:
  0.0 84.6 jit_solution(7324754546041861549)
XLA Ops:
  0.6 3.4 %lines_out.1 = (bf16[32,16,256]{2,1,0:T(8,128)(2,1)}, bf16[2,2,192,128]{3,2,1,0:T(8,128)(2,1)}) custom-call(f32[2,2,192,128]{3,2,1,0:T(8,128)} %bitcast.10, f32[8,2,192,128]{3,2,1,0:T(8,128)} %beta_hbm.3, s32[1,128]{1,0:T(1,128)} %bitcast.16, bf16[2,512,384]{2,1,0:T(8,128)(2,1)} %constant.27.clone.table_hbm), custom_call_target="tpu_custom_call" | custom-call | tf_op jit(solution)/shard_map/lines_out/pallas_call | solution.py:611
  4.1 6.7 %all-to-all-start = ((bf16[32,16,256]{2,1,0:T(8,128)(2,1)}), bf16[32,16,256]{2,1,0:T(8,128)(2,1)}, u32[]{:S(2)}, u32[]{:S(2)}) async-start(bf16[32,16,256]{2,1,0:T(8,128)(2,1)} %get-tuple-element.13), calls=%async_computation | async-start | bytes 524288 | tf_op jit(solution)/shard_map/all_to_all | solution.py:545
  10.8 3.7 %collective-permute-start.3 = (bf16[2,2,192,128]{3,2,1,0:T(8,128)(2,1)}, bf16[2,2,192,128]{3,2,1,0:T(8,128)(2,1)}, u32[]{:S(2)}, u32[]{:S(2)}) collective-permute-start(bf16[2,2,192,128]{3,2,1,0:T(8,128)(2,1)} %get-tuple-element.15), channel_id=1, source_target_pairs={{0,192},{32,224},{64,0},{96,32},{128,64},{160,96},{192,128},{224,1... | collective-permute-start | bytes 589832 | tf_op jit(solution)/shard_map/ppermute | solution.py:537
  14.5 0.9 %collective-permute-start.2 = (bf16[2,2,192,128]{3,2,1,0:T(8,128)(2,1)}, bf16[2,2,192,128]{3,2,1,0:T(8,128)(2,1)}, u32[]{:S(2)}, u32[]{:S(2)}) collective-permute-start(bf16[2,2,192,128]{3,2,1,0:T(8,128)(2,1)} %get-tuple-element.15), channel_id=1, source_target_pairs={{0,224},{32,0},{64,32},{96,64},{128,96},{160,128},{192,160},{224,1... | collective-permute-start | bytes 589832 | tf_op jit(solution)/shard_map/ppermute | solution.py:537
  15.4 0.6 collective-permute-start.1
  16.0 0.6 collective-permute-start
  16.6 18.0 %all-to-all-done = bf16[32,16,256]{2,1,0:T(8,128)(2,1)} async-done(((bf16[32,16,256]{2,1,0:T(8,128)(2,1)}), bf16[32,16,256]{2,1,0:T(8,128)(2,1)}, u32[]{:S(2)}, u32[]{:S(2)}) %all-to-all-start) | async-done | bytes 262176 | tf_op jit(solution)/shard_map/all_to_all | solution.py:545
  34.6 18.8 %planes.1 = (bf16[512,256]{1,0:T(8,128)(2,1)}, f32[32,128]{1,0:T(8,128)}) custom-call(bf16[512,256]{1,0:T(8,128)(2,1)} %bitcast.2.recv_hbm, f32[6,192,192]{2,1,0:T(8,128)} %pot_hbm.1, bf16[8,256,256]{2,1,0:T(8,128)(2,1)} %constant.20.clone.spread_hbm, bf16[384,192]{1,0:T(8,128)(2,1)} %constant.21.clone.y_hbm, bf16[128,256]{1,0:T(8,128)(2,1)} %constant.22.clone.mix_in_hbm, ...), custom_call_target="tpu_custom_call" | custom-call | flops 20000000000 | bytes 4194304 | tf_op jit(solution)/shard_map/planes/pallas_call | solution.py:549
  53.4 0.0 collective-permute-done.3.other_3
  53.4 0.0 collective-permute-done.2.other_2
  53.4 0.0 collective-permute-done.1.other_1
  53.4 0.0 collective-permute-done.other_0
  53.4 15.6 %all_to_all.22 = bf16[32,16,256]{2,1,0:T(8,128)(2,1)} all-to-all(bf16[32,16,256]{2,1,0:T(8,128)(2,1)} %bitcast.13), channel_id=1, replica_groups=mesh['band'=8,'pw'=32] {'pw'}, dimensions={0} | all-to-all | bytes 524288 | tf_op jit(solution)/shard_map/all_to_all | solution.py:545
  69.0 3.6 %lines_in.1 = (f32[2,2,192,128]{3,2,1,0:T(8,128)}, f32[32,128]{1,0:T(8,128)}) custom-call(bf16[512,256]{1,0:T(8,128)(2,1)} %bitcast.12, bf16[2,384,512]{2,1,0:T(8,128)(2,1)} %constant.28.clone.table_hbm, f32[2,2,192,128]{3,2,1,0:T(8,128)} %bitcast.11, f32[8,2,192,128]{3,2,1,0:T(8,128)} %beta_hbm.3, f32[32,128]{1,0:T(8,128)} %get-tuple-element.17.mixed_hbm, ...), custom_call_target="tpu_custom_call" | custom-call | tf_op jit(solution)/shard_map/lines_in/pallas_call | solution.py:638
  72.6 11.1 %all_to_all.23 = f32[32,1,128]{2,1,0:T(1,128)S(1)} all-to-all(f32[32,1,128]{2,1,0:T(1,128)} %bitcast.15), channel_id=1, replica_groups=mesh['band'=8,'pw'=32] {'pw'}, dimensions={0} | all-to-all | bytes 32768 | tf_op jit(solution)/shard_map/all_to_all | solution.py:545
  83.8 0.1 broadcast_in_dim_reshape.3
  83.8 0.7 copy.19
  (1 shorter events, 0.0 us)
Async XLA Ops:
  4.1 30.5 %all-to-all-start = ((bf16[32,16,256]{2,1,0:T(8,128)(2,1)}), bf16[32,16,256]{2,1,0:T(8,128)(2,1)}, u32[]{:S(2)}, u32[]{:S(2)}) async-start(bf16[32,16,256]{2,1,0:T(8,128)(2,1)} %get-tuple-element.13), calls=%async_computation | async-start | bytes 524288 | tf_op jit(solution)/shard_map/all_to_all | solution.py:545
  10.8 42.6 %collective-permute-start.3 = (bf16[2,2,192,128]{3,2,1,0:T(8,128)(2,1)}, bf16[2,2,192,128]{3,2,1,0:T(8,128)(2,1)}, u32[]{:S(2)}, u32[]{:S(2)}) collective-permute-start(bf16[2,2,192,128]{3,2,1,0:T(8,128)(2,1)} %get-tuple-element.15), channel_id=1, source_target_pairs={{0,192},{32,224},{64,0},{96,32},{128,64},{160,96},{192,128},{224,1... | collective-permute-start | bytes 589832 | tf_op jit(solution)/shard_map/ppermute | solution.py:537
  14.5 38.9 %collective-permute-start.2 = (bf16[2,2,192,128]{3,2,1,0:T(8,128)(2,1)}, bf16[2,2,192,128]{3,2,1,0:T(8,128)(2,1)}, u32[]{:S(2)}, u32[]{:S(2)}) collective-permute-start(bf16[2,2,192,128]{3,2,1,0:T(8,128)(2,1)} %get-tuple-element.15), channel_id=1, source_target_pairs={{0,224},{32,0},{64,32},{96,64},{128,96},{160,128},{192,160},{224,1... | collective-permute-start | bytes 589832 | tf_op jit(solution)/shard_map/ppermute | solution.py:537
  15.4 38.1 %collective-permute-start.1 = (bf16[2,2,192,128]{3,2,1,0:T(8,128)(2,1)}, bf16[2,2,192,128]{3,2,1,0:T(8,128)(2,1)}, u32[]{:S(2)}, u32[]{:S(2)}) collective-permute-start(bf16[2,2,192,128]{3,2,1,0:T(8,128)(2,1)} %get-tuple-element.15), channel_id=1, source_target_pairs={{0,32},{32,64},{64,96},{96,128},{128,160},{160,192},{192,224},{224... | collective-permute-start | bytes 589832 | tf_op jit(solution)/shard_map/ppermute | solution.py:537
  16.0 37.5 %collective-permute-start = (bf16[2,2,192,128]{3,2,1,0:T(8,128)(2,1)}, bf16[2,2,192,128]{3,2,1,0:T(8,128)(2,1)}, u32[]{:S(2)}, u32[]{:S(2)}) collective-permute-start(bf16[2,2,192,128]{3,2,1,0:T(8,128)(2,1)} %get-tuple-element.15), channel_id=1, source_target_pairs={{0,64},{32,96},{64,128},{96,160},{128,192},{160,224},{192,0},{224,... | collective-permute-start | bytes 589832 | tf_op jit(solution)/shard_map/ppermute | solution.py:537

commit v6 on v5

--- a/solution.py
+++ b/solution.py
@@ -567,15 +567,15 @@
         ]
         + [
             pltpu.VMEM((PW * ROWS, 2 * LANES), BF),
-            pltpu.VMEM((COLS, LANES), F32),
-            pltpu.VMEM((COLS, LANES), F32),
-            pltpu.VMEM((SPAN * GRID, LANES), F32),
-            pltpu.VMEM((SPAN * STEP, LANES), F32),
-            pltpu.VMEM((SPAN * STEP, LANES), F32),
-            pltpu.VMEM((SPAN * STEP, LANES), F32),
-            pltpu.VMEM((SPAN * STEP, LANES), F32),
-            pltpu.VMEM((DEPTH * GRID, LANES), F32),
-            pltpu.VMEM((DEPTH * GRID, LANES), F32),
+            pltpu.VMEM((COLS + 8, LANES), F32),
+            pltpu.VMEM((COLS + 8, LANES), F32),
+            pltpu.VMEM((SPAN * GRID + 8, LANES), F32),
+            pltpu.VMEM(((SPAN + 1) * STEP + 7, LANES), F32),
+            pltpu.VMEM(((SPAN + 1) * STEP + 7, LANES), F32),
+            pltpu.VMEM(((SPAN + 1) * STEP + 7, LANES), F32),
+            pltpu.VMEM(((SPAN + 1) * STEP + 7, LANES), F32),
+            pltpu.VMEM((DEPTH * GRID + 8, LANES), F32),
+            pltpu.VMEM((DEPTH * GRID + 8, LANES), F32),
             pltpu.VMEM((PW, LOCAL), jnp.int32),
             pltpu.SMEM((PW, LOCAL), jnp.int32),
             pltpu.SemaphoreType.DMA((15,)),

time: 84.9 us -> 84.9 us (level)
  no operation moved by 1% of the time
where the time goes in v6:
time: 84.9 us; the launch traced here: 84.6 us
  blocking collectives  26.7 us (31%)
  Pallas kernels  25.8 us (30%)
  waiting for transfers between devices  18 us (21%)
  starting transfers between devices  12.5 us (15%)
    all_to_all x2, blocking collectives, exchange(): return lax.all_to_all(value, 'pw', split_axis=0, concat_axis=0, tiled=True)  26.7 us
    pallas_call x1, Pallas kernels, planes_call(): pl.pallas_call(planes_kernel, name=name, out_shape=(jax.ShapeDtypeStruct(...  18.8 us
    all_to_all x1, waiting for transfers between devices, exchange(): return lax.all_to_all(value, 'pw', split_axis=0, concat_axis=0, tiled=True)  18 us
    all_to_all x1, starting transfers between devices, exchange(): return lax.all_to_all(value, 'pw', split_axis=0, concat_axis=0, tiled=True)  6.73 us
    ppermute x4, starting transfers between devices, around(): lax.ppermute(value, axis, [(s, (s + steps) % count) for s in range(count)])  5.8 us
    pallas_call x1, Pallas kernels, per_device(): pl.pallas_call(finish_kernel, name='lines_in', out_shape=(jax.ShapeDtypeS...  3.58 us
    pallas_call x1, Pallas kernels, per_device(): pl.pallas_call(send_kernel, name='lines_out', out_shape=(jax.ShapeDtypeSt...  3.42 us
  transfers between devices with their start and end apart: 5, of which 1 were waited for; matrix products, arithmetic and copies ran while one was open for 0% of the time, Pallas kernels for 22%

profile of v6, /device:TPU:129, one launch (start us, length us, event | category | flops | bytes accessed | tf_op | source)
XLA Modules:
  0.0 84.6 jit_solution(5833952105029473006)
XLA Ops:
  0.6 3.4 %lines_out.1 = (bf16[32,16,256]{2,1,0:T(8,128)(2,1)}, bf16[2,2,192,128]{3,2,1,0:T(8,128)(2,1)}) custom-call(f32[2,2,192,128]{3,2,1,0:T(8,128)} %bitcast.10, f32[8,2,192,128]{3,2,1,0:T(8,128)} %beta_hbm.3, s32[1,128]{1,0:T(1,128)} %bitcast.16, bf16[2,512,384]{2,1,0:T(8,128)(2,1)} %constant.27.clone.table_hbm), custom_call_target="tpu_custom_call" | custom-call | tf_op jit(solution)/shard_map/lines_out/pallas_call | solution.py:611
  4.1 6.7 %all-to-all-start = ((bf16[32,16,256]{2,1,0:T(8,128)(2,1)}), bf16[32,16,256]{2,1,0:T(8,128)(2,1)}, u32[]{:S(2)}, u32[]{:S(2)}) async-start(bf16[32,16,256]{2,1,0:T(8,128)(2,1)} %get-tuple-element.13), calls=%async_computation | async-start | bytes 524288 | tf_op jit(solution)/shard_map/all_to_all | solution.py:545
  10.8 3.7 %collective-permute-start.3 = (bf16[2,2,192,128]{3,2,1,0:T(8,128)(2,1)}, bf16[2,2,192,128]{3,2,1,0:T(8,128)(2,1)}, u32[]{:S(2)}, u32[]{:S(2)}) collective-permute-start(bf16[2,2,192,128]{3,2,1,0:T(8,128)(2,1)} %get-tuple-element.15), channel_id=1, source_target_pairs={{0,192},{32,224},{64,0},{96,32},{128,64},{160,96},{192,128},{224,1... | collective-permute-start | bytes 589832 | tf_op jit(solution)/shard_map/ppermute | solution.py:537
  14.5 0.9 %collective-permute-start.2 = (bf16[2,2,192,128]{3,2,1,0:T(8,128)(2,1)}, bf16[2,2,192,128]{3,2,1,0:T(8,128)(2,1)}, u32[]{:S(2)}, u32[]{:S(2)}) collective-permute-start(bf16[2,2,192,128]{3,2,1,0:T(8,128)(2,1)} %get-tuple-element.15), channel_id=1, source_target_pairs={{0,224},{32,0},{64,32},{96,64},{128,96},{160,128},{192,160},{224,1... | collective-permute-start | bytes 589832 | tf_op jit(solution)/shard_map/ppermute | solution.py:537
  15.4 0.6 collective-permute-start.1
  16.0 0.6 collective-permute-start
  16.6 18.0 %all-to-all-done = bf16[32,16,256]{2,1,0:T(8,128)(2,1)} async-done(((bf16[32,16,256]{2,1,0:T(8,128)(2,1)}), bf16[32,16,256]{2,1,0:T(8,128)(2,1)}, u32[]{:S(2)}, u32[]{:S(2)}) %all-to-all-start) | async-done | bytes 262176 | tf_op jit(solution)/shard_map/all_to_all | solution.py:545
  34.6 18.8 %planes.1 = (bf16[512,256]{1,0:T(8,128)(2,1)}, f32[32,128]{1,0:T(8,128)}) custom-call(bf16[512,256]{1,0:T(8,128)(2,1)} %bitcast.2.recv_hbm, f32[6,192,192]{2,1,0:T(8,128)} %pot_hbm.1, bf16[8,256,256]{2,1,0:T(8,128)(2,1)} %constant.20.clone.spread_hbm, bf16[384,192]{1,0:T(8,128)(2,1)} %constant.21.clone.y_hbm, bf16[128,256]{1,0:T(8,128)(2,1)} %constant.22.clone.mix_in_hbm, ...), custom_call_target="tpu_custom_call" | custom-call | flops 20000000000 | bytes 4194304 | tf_op jit(solution)/shard_map/planes/pallas_call | solution.py:549
  53.4 0.0 collective-permute-done.3.other_3
  53.4 0.0 collective-permute-done.2.other_2
  53.4 0.0 collective-permute-done.1.other_1
  53.4 0.0 collective-permute-done.other_0
  53.4 15.6 %all_to_all.22 = bf16[32,16,256]{2,1,0:T(8,128)(2,1)} all-to-all(bf16[32,16,256]{2,1,0:T(8,128)(2,1)} %bitcast.13), channel_id=1, replica_groups=mesh['band'=8,'pw'=32] {'pw'}, dimensions={0} | all-to-all | bytes 524288 | tf_op jit(solution)/shard_map/all_to_all | solution.py:545
  69.0 3.6 %lines_in.1 = (f32[2,2,192,128]{3,2,1,0:T(8,128)}, f32[32,128]{1,0:T(8,128)}) custom-call(bf16[512,256]{1,0:T(8,128)(2,1)} %bitcast.12, bf16[2,384,512]{2,1,0:T(8,128)(2,1)} %constant.28.clone.table_hbm, f32[2,2,192,128]{3,2,1,0:T(8,128)} %bitcast.11, f32[8,2,192,128]{3,2,1,0:T(8,128)} %beta_hbm.3, f32[32,128]{1,0:T(8,128)} %get-tuple-element.17.mixed_hbm, ...), custom_call_target="tpu_custom_call" | custom-call | tf_op jit(solution)/shard_map/lines_in/pallas_call | solution.py:638
  72.6 11.1 %all_to_all.23 = f32[32,1,128]{2,1,0:T(1,128)S(1)} all-to-all(f32[32,1,128]{2,1,0:T(1,128)} %bitcast.15), channel_id=1, replica_groups=mesh['band'=8,'pw'=32] {'pw'}, dimensions={0} | all-to-all | bytes 32768 | tf_op jit(solution)/shard_map/all_to_all | solution.py:545
  83.8 0.1 broadcast_in_dim_reshape.3
  83.8 0.7 copy.19
  (1 shorter events, 0.0 us)
Async XLA Ops:
  4.1 30.5 %all-to-all-start = ((bf16[32,16,256]{2,1,0:T(8,128)(2,1)}), bf16[32,16,256]{2,1,0:T(8,128)(2,1)}, u32[]{:S(2)}, u32[]{:S(2)}) async-start(bf16[32,16,256]{2,1,0:T(8,128)(2,1)} %get-tuple-element.13), calls=%async_computation | async-start | bytes 524288 | tf_op jit(solution)/shard_map/all_to_all | solution.py:545
  10.8 42.6 %collective-permute-start.3 = (bf16[2,2,192,128]{3,2,1,0:T(8,128)(2,1)}, bf16[2,2,192,128]{3,2,1,0:T(8,128)(2,1)}, u32[]{:S(2)}, u32[]{:S(2)}) collective-permute-start(bf16[2,2,192,128]{3,2,1,0:T(8,128)(2,1)} %get-tuple-element.15), channel_id=1, source_target_pairs={{0,192},{32,224},{64,0},{96,32},{128,64},{160,96},{192,128},{224,1... | collective-permute-start | bytes 589832 | tf_op jit(solution)/shard_map/ppermute | solution.py:537
  14.5 38.9 %collective-permute-start.2 = (bf16[2,2,192,128]{3,2,1,0:T(8,128)(2,1)}, bf16[2,2,192,128]{3,2,1,0:T(8,128)(2,1)}, u32[]{:S(2)}, u32[]{:S(2)}) collective-permute-start(bf16[2,2,192,128]{3,2,1,0:T(8,128)(2,1)} %get-tuple-element.15), channel_id=1, source_target_pairs={{0,224},{32,0},{64,32},{96,64},{128,96},{160,128},{192,160},{224,1... | collective-permute-start | bytes 589832 | tf_op jit(solution)/shard_map/ppermute | solution.py:537
  15.4 38.1 %collective-permute-start.1 = (bf16[2,2,192,128]{3,2,1,0:T(8,128)(2,1)}, bf16[2,2,192,128]{3,2,1,0:T(8,128)(2,1)}, u32[]{:S(2)}, u32[]{:S(2)}) collective-permute-start(bf16[2,2,192,128]{3,2,1,0:T(8,128)(2,1)} %get-tuple-element.15), channel_id=1, source_target_pairs={{0,32},{32,64},{64,96},{96,128},{128,160},{160,192},{192,224},{224... | collective-permute-start | bytes 589832 | tf_op jit(solution)/shard_map/ppermute | solution.py:537
  16.0 37.5 %collective-permute-start = (bf16[2,2,192,128]{3,2,1,0:T(8,128)(2,1)}, bf16[2,2,192,128]{3,2,1,0:T(8,128)(2,1)}, u32[]{:S(2)}, u32[]{:S(2)}) collective-permute-start(bf16[2,2,192,128]{3,2,1,0:T(8,128)(2,1)} %get-tuple-element.15), channel_id=1, source_target_pairs={{0,64},{32,96},{64,128},{96,160},{128,192},{160,224},{192,0},{224,... | collective-permute-start | bytes 589832 | tf_op jit(solution)/shard_map/ppermute | solution.py:537

commit v7 on v6

--- a/solution.py
+++ b/solution.py
@@ -93,10 +93,10 @@
     for g in range(GROUPS):
         c, s = cos[:SPAN, g::GROUPS] / balance, sin[:SPAN, g::GROUPS] / balance
         x_inverse[g] = side_by_side(np.block([[c.T, -s.T], [s.T, c.T]]))
-        x_forward[g] = side_by_side(np.block([[c, s], [-s, c]]))
+        x_forward[g] = side_by_side(np.block([[c, s], [-s, c]]) / balance)
     return dict(
         to_planes=to_planes,
-        from_planes=from_planes,
+        from_planes=from_planes * balance,
         spread=spread,
         y_table=np.concatenate([cos, sin], axis=0) * balance,
         mix_in=mix_in,
@@ -475,7 +475,7 @@
     fxy = fx * fx + fy * fy
     back_copy.wait()
     table_copy.wait()
-    local_ref[...] = dot(table_ref[0], back_ref[...]) + dot(table_ref[1], back_ref[...])
+    local_ref[...] = dot(table_ref[...], back_ref[...])
     totals = [jnp.zeros((8, LANES), F32) for _ in range(32)]
     outs = []
     for k, start in enumerate(steps):
@@ -632,7 +632,9 @@
     others = [around(low_orbitals, "band", -offset) for offset in OFFSETS]
 
     back, mixed = planes_call(recv.reshape(PW * ROWS, 2 * LANES), potential, half, coupling)
-    back, others = lax.optimization_barrier((back, others))
+    order = (1, 0, 2, 3)
+    back, *held = lax.optimization_barrier((back, *(others[o] for o in order)))
+    others = [held[order.index(o)] for o in range(4)]
     returned = exchange(back.reshape(PW, ROWS, 2 * LANES)).reshape(PW * ROWS, 2 * LANES)
 
     applied, cross = pl.pallas_call(
@@ -649,7 +651,7 @@
             pltpu.VMEM((1, LOCAL), jnp.int32),
             pltpu.VMEM((PW, LANES), F32),
             pltpu.VMEM((PW * ROWS, 2 * LANES), BF),
-            pltpu.VMEM((2, 2 * GRID, PW * ROWS), BF),
+            pltpu.VMEM((2 * GRID, PW * ROWS), BF),
             pltpu.VMEM((BANDS, 2, GRID, LOCAL), F32),
             pltpu.VMEM((PROJ, 2, GRID, LOCAL), F32),
             pltpu.VMEM((4, BANDS, 2, GRID, LOCAL), BF),
@@ -660,7 +662,7 @@
         compiler_params=pltpu.CompilerParams(vmem_limit_bytes=64 << 20),
     )(
         returned,
-        two_parts(tables["from_planes"]),
+        half["from_planes"],
         block,
         projectors,
         mixed,

time: 84.9 us -> 84.7 us (level)
  no operation moved by 1% of the time
where the time goes in v7:
time: 84.7 us; the launch traced here: 84.3 us
  blocking collectives  26.7 us (32%)
  Pallas kernels  25.6 us (30%)
  waiting for transfers between devices  18 us (21%)
  starting transfers between devices  12.5 us (15%)
    all_to_all x2, blocking collectives, exchange(): return lax.all_to_all(value, 'pw', split_axis=0, concat_axis=0, tiled=True)  26.7 us
    pallas_call x1, Pallas kernels, planes_call(): pl.pallas_call(planes_kernel, name=name, out_shape=(jax.ShapeDtypeStruct(...  18.8 us
    all_to_all x1, waiting for transfers between devices, exchange(): return lax.all_to_all(value, 'pw', split_axis=0, concat_axis=0, tiled=True)  18 us
    all_to_all x1, starting transfers between devices, exchange(): return lax.all_to_all(value, 'pw', split_axis=0, concat_axis=0, tiled=True)  6.73 us
    ppermute x4, starting transfers between devices, around(): lax.ppermute(value, axis, [(s, (s + steps) % count) for s in range(count)])  5.8 us
    pallas_call x1, Pallas kernels, per_device(): pl.pallas_call(send_kernel, name='lines_out', out_shape=(jax.ShapeDtypeSt...  3.42 us
    pallas_call x1, Pallas kernels, per_device(): pl.pallas_call(finish_kernel, name='lines_in', out_shape=(jax.ShapeDtypeS...  3.37 us
  transfers between devices with their start and end apart: 5, of which 1 were waited for; matrix products, arithmetic and copies ran while one was open for 0% of the time, Pallas kernels for 22%

profile of v7, /device:TPU:129, one launch (start us, length us, event | category | flops | bytes accessed | tf_op | source)
XLA Modules:
  0.0 84.3 jit_solution(1739804773534474529)
XLA Ops:
  0.6 3.4 %lines_out.1 = (bf16[32,16,256]{2,1,0:T(8,128)(2,1)}, bf16[2,2,192,128]{3,2,1,0:T(8,128)(2,1)}) custom-call(f32[2,2,192,128]{3,2,1,0:T(8,128)} %bitcast.10, f32[8,2,192,128]{3,2,1,0:T(8,128)} %beta_hbm.3, s32[1,128]{1,0:T(1,128)} %bitcast.16, bf16[2,512,384]{2,1,0:T(8,128)(2,1)} %constant.28.clone.table_hbm), custom_call_target="tpu_custom_call" | custom-call | tf_op jit(solution)/shard_map/lines_out/pallas_call | solution.py:611
  4.1 6.7 %all-to-all-start = ((bf16[32,16,256]{2,1,0:T(8,128)(2,1)}), bf16[32,16,256]{2,1,0:T(8,128)(2,1)}, u32[]{:S(2)}, u32[]{:S(2)}) async-start(bf16[32,16,256]{2,1,0:T(8,128)(2,1)} %get-tuple-element.13), calls=%async_computation | async-start | bytes 524288 | tf_op jit(solution)/shard_map/all_to_all | solution.py:545
  10.8 3.7 %collective-permute-start.3 = (bf16[2,2,192,128]{3,2,1,0:T(8,128)(2,1)}, bf16[2,2,192,128]{3,2,1,0:T(8,128)(2,1)}, u32[]{:S(2)}, u32[]{:S(2)}) collective-permute-start(bf16[2,2,192,128]{3,2,1,0:T(8,128)(2,1)} %get-tuple-element.15), channel_id=1, source_target_pairs={{0,192},{32,224},{64,0},{96,32},{128,64},{160,96},{192,128},{224,1... | collective-permute-start | bytes 589832 | tf_op jit(solution)/shard_map/ppermute | solution.py:537
  14.5 0.9 %collective-permute-start.2 = (bf16[2,2,192,128]{3,2,1,0:T(8,128)(2,1)}, bf16[2,2,192,128]{3,2,1,0:T(8,128)(2,1)}, u32[]{:S(2)}, u32[]{:S(2)}) collective-permute-start(bf16[2,2,192,128]{3,2,1,0:T(8,128)(2,1)} %get-tuple-element.15), channel_id=1, source_target_pairs={{0,224},{32,0},{64,32},{96,64},{128,96},{160,128},{192,160},{224,1... | collective-permute-start | bytes 589832 | tf_op jit(solution)/shard_map/ppermute | solution.py:537
  15.4 1.2 %collective-permute-start.1 = (bf16[2,2,192,128]{3,2,1,0:T(8,128)(2,1)}, bf16[2,2,192,128]{3,2,1,0:T(8,128)(2,1)}, u32[]{:S(2)}, u32[]{:S(2)}) collective-permute-start(bf16[2,2,192,128]{3,2,1,0:T(8,128)(2,1)} %get-tuple-element.15), channel_id=1, source_target_pairs={{0,64},{32,96},{64,128},{96,160},{128,192},{160,224},{192,0},{224,... | collective-permute-start | bytes 589832 | tf_op jit(solution)/shard_map/ppermute | solution.py:537
  16.6 0.0 collective-permute-start
  16.6 18.0 %all-to-all-done = bf16[32,16,256]{2,1,0:T(8,128)(2,1)} async-done(((bf16[32,16,256]{2,1,0:T(8,128)(2,1)}), bf16[32,16,256]{2,1,0:T(8,128)(2,1)}, u32[]{:S(2)}, u32[]{:S(2)}) %all-to-all-start) | async-done | bytes 262176 | tf_op jit(solution)/shard_map/all_to_all | solution.py:545
  34.6 18.8 %planes.1 = (bf16[512,256]{1,0:T(8,128)(2,1)}, f32[32,128]{1,0:T(8,128)}) custom-call(bf16[512,256]{1,0:T(8,128)(2,1)} %bitcast.2.recv_hbm, f32[6,192,192]{2,1,0:T(8,128)} %pot_hbm.1, bf16[8,256,256]{2,1,0:T(8,128)(2,1)} %constant.21.clone.spread_hbm, bf16[384,192]{1,0:T(8,128)(2,1)} %constant.22.clone.y_hbm, bf16[128,256]{1,0:T(8,128)(2,1)} %constant.23.clone.mix_in_hbm, ...), custom_call_target="tpu_custom_call" | custom-call | flops 20000000000 | bytes 4194304 | tf_op jit(solution)/shard_map/planes/pallas_call | solution.py:549
  53.4 0.0 collective-permute-done.3.other_3
  53.4 0.0 collective-permute-done.2.other_2
  53.4 0.0 collective-permute-done.1.other_0
  53.4 0.0 collective-permute-done.other_1
  53.4 15.6 %all_to_all.22 = bf16[32,16,256]{2,1,0:T(8,128)(2,1)} all-to-all(bf16[32,16,256]{2,1,0:T(8,128)(2,1)} %bitcast.13), channel_id=1, replica_groups=mesh['band'=8,'pw'=32] {'pw'}, dimensions={0} | all-to-all | bytes 524288 | tf_op jit(solution)/shard_map/all_to_all | solution.py:545
  69.0 3.4 %lines_in.1 = (f32[2,2,192,128]{3,2,1,0:T(8,128)}, f32[32,128]{1,0:T(8,128)}) custom-call(bf16[512,256]{1,0:T(8,128)(2,1)} %bitcast.12, bf16[384,512]{1,0:T(8,128)(2,1)} %constant.20.clone.table_hbm, f32[2,2,192,128]{3,2,1,0:T(8,128)} %bitcast.11, f32[8,2,192,128]{3,2,1,0:T(8,128)} %beta_hbm.3, f32[32,128]{1,0:T(8,128)} %get-tuple-element.17.mixed_hbm, ...), custom_call_target="tpu_custom_call" | custom-call | tf_op jit(solution)/shard_map/lines_in/pallas_call | solution.py:640
  72.4 11.1 %all_to_all.23 = f32[32,1,128]{2,1,0:T(1,128)S(1)} all-to-all(f32[32,1,128]{2,1,0:T(1,128)} %bitcast.15), channel_id=1, replica_groups=mesh['band'=8,'pw'=32] {'pw'}, dimensions={0} | all-to-all | bytes 32768 | tf_op jit(solution)/shard_map/all_to_all | solution.py:545
  83.5 0.1 broadcast_in_dim_reshape.3
  83.6 0.7 copy.19
  (1 shorter events, 0.0 us)
Async XLA Ops:
  4.1 30.5 %all-to-all-start = ((bf16[32,16,256]{2,1,0:T(8,128)(2,1)}), bf16[32,16,256]{2,1,0:T(8,128)(2,1)}, u32[]{:S(2)}, u32[]{:S(2)}) async-start(bf16[32,16,256]{2,1,0:T(8,128)(2,1)} %get-tuple-element.13), calls=%async_computation | async-start | bytes 524288 | tf_op jit(solution)/shard_map/all_to_all | solution.py:545
  10.8 42.6 %collective-permute-start.3 = (bf16[2,2,192,128]{3,2,1,0:T(8,128)(2,1)}, bf16[2,2,192,128]{3,2,1,0:T(8,128)(2,1)}, u32[]{:S(2)}, u32[]{:S(2)}) collective-permute-start(bf16[2,2,192,128]{3,2,1,0:T(8,128)(2,1)} %get-tuple-element.15), channel_id=1, source_target_pairs={{0,192},{32,224},{64,0},{96,32},{128,64},{160,96},{192,128},{224,1... | collective-permute-start | bytes 589832 | tf_op jit(solution)/shard_map/ppermute | solution.py:537
  14.5 38.9 %collective-permute-start.2 = (bf16[2,2,192,128]{3,2,1,0:T(8,128)(2,1)}, bf16[2,2,192,128]{3,2,1,0:T(8,128)(2,1)}, u32[]{:S(2)}, u32[]{:S(2)}) collective-permute-start(bf16[2,2,192,128]{3,2,1,0:T(8,128)(2,1)} %get-tuple-element.15), channel_id=1, source_target_pairs={{0,224},{32,0},{64,32},{96,64},{128,96},{160,128},{192,160},{224,1... | collective-permute-start | bytes 589832 | tf_op jit(solution)/shard_map/ppermute | solution.py:537
  15.4 38.1 %collective-permute-start.1 = (bf16[2,2,192,128]{3,2,1,0:T(8,128)(2,1)}, bf16[2,2,192,128]{3,2,1,0:T(8,128)(2,1)}, u32[]{:S(2)}, u32[]{:S(2)}) collective-permute-start(bf16[2,2,192,128]{3,2,1,0:T(8,128)(2,1)} %get-tuple-element.15), channel_id=1, source_target_pairs={{0,64},{32,96},{64,128},{96,160},{128,192},{160,224},{192,0},{224,... | collective-permute-start | bytes 589832 | tf_op jit(solution)/shard_map/ppermute | solution.py:537
  16.6 36.8 %collective-permute-start = (bf16[2,2,192,128]{3,2,1,0:T(8,128)(2,1)}, bf16[2,2,192,128]{3,2,1,0:T(8,128)(2,1)}, u32[]{:S(2)}, u32[]{:S(2)}) collective-permute-start(bf16[2,2,192,128]{3,2,1,0:T(8,128)(2,1)} %get-tuple-element.15), channel_id=1, source_target_pairs={{0,32},{32,64},{64,96},{96,128},{128,160},{160,192},{192,224},{224... | collective-permute-start | bytes 589832 | tf_op jit(solution)/shard_map/ppermute | solution.py:537
